TPU v7x, 128 devices: a whole 4x4x4 slice. The times are simulated.
128 devices in a mesh: dp: 32 (over z, y, core), tensor: 4 (over x).
Axes of the slice: x: 4, y: 4, z: 4, core: 2. Of those that a mesh axis runs over, the one named last changes fastest.
Arguments:
- old_weights: float32 [3, 1024, 16384], P(None, ('dp', 'tensor')), may hold values from -0.046875 to 0.046875
- old_first: float32 [3, 1024, 16384], P(None, ('dp', 'tensor')), may hold values from -6 to 6
- old_second: float32 [3, 1024, 16384], P(None, ('dp', 'tensor')), may hold values from 0.01 to 1
- old_blocks: int32 [128], replicated, may hold values from 0 to 2, as said below
- owner_map: int32 [128, 4], replicated, may hold values from 0 to 3, each once within a row
- inputs: bfloat16 [2, 7680, 16384], P(None, 'dp', 'tensor'), may hold values from -6 to 6
- cotangent: bfloat16 [2, 7680, 16384], P(None, 'dp'), may hold values from -0.19921875 to 0.19921875
Outputs:
- new_weights: float32 [16384, 3, 512], P('dp', None, 'tensor')
- new_first: float32 [16384, 3, 512], P('dp', None, 'tensor')
- new_second: float32 [16384, 3, 512], P('dp', None, 'tensor')
Inputs may be any that keep to these rules, and one draw needn't show every extreme that they name: `old_blocks`: pairs of old shards (2 p, 2 p + 1) together hold 2 groups; the counts sum to 128; shard 0 holds 2.
All inputs are finite; a program needn't handle non-finite values.
Results may differ from a plain program's by a relative error of at most 0.03.
Values may be sent and summed in bfloat16 or wider, within the bound.
A program may use at most 128 MiB of HBM per device.

v0:
```python
import jax
import jax.numpy as jnp
from jax import lax
from jax.sharding import PartitionSpec as P


def silu_parts(gate):
    sig = jax.nn.sigmoid(gate)
    return (gate * sig, sig * (1.0 + gate * (1.0 - sig)))


def contract_rows(left, right):
    return lax.dot_general(
        left, right, (((0,), (0,)), ((), ())), preferred_element_type=jnp.float32
    )


def on_device(old_weights, old_first, old_second, old_blocks, owner_map, inputs, cotangent):
    members = lax.axis_size("tensor")
    lanes = lax.axis_size("dp")
    shards = members * lanes
    slot_units = old_weights.shape[1]
    capacity = slot_units // members
    width = old_weights.shape[2]
    rows = width // lanes
    groups = owner_map.shape[0]
    myself = lax.axis_index("dp") * members + lax.axis_index("tensor")
    ends = jnp.cumsum(old_blocks)
    starts = ends - old_blocks
    padded_map = jnp.concatenate([owner_map, jnp.zeros((capacity, members), jnp.int32)], axis=0)
    local_map = lax.dynamic_slice_in_dim(padded_map, starts[myself], capacity, 0)
    living = jnp.arange(capacity, dtype=jnp.int32) < old_blocks[myself]
    owners = jnp.arange(members, dtype=jnp.int32)
    picked = (local_map[:, None, :] == owners[None, :, None]) & living[:, None, None]

    def outgoing(old):
        pieces = old.reshape(3, capacity, members, width)
        chosen = jnp.sum(
            jnp.where(picked[None, :, :, :, None], pieces[:, :, None, :, :], 0.0), axis=3
        )
        chosen = chosen.reshape(3, capacity, members, lanes, rows)
        return jnp.transpose(chosen, (4, 0, 3, 2, 1)).reshape(rows, 3, shards * capacity)

    sent = (outgoing(old_weights), outgoing(old_first), outgoing(old_second))
    arrived = (
        lax.all_to_all(
            sent[0].astype(jnp.bfloat16), ("dp", "tensor"), split_axis=2, concat_axis=2, tiled=True
        ).astype(jnp.float32),
        lax.all_to_all(
            sent[1].astype(jnp.bfloat16), ("dp", "tensor"), split_axis=2, concat_axis=2, tiled=True
        ).astype(jnp.float32),
        lax.all_to_all(
            sent[2].astype(jnp.bfloat16), ("dp", "tensor"), split_axis=2, concat_axis=2, tiled=True
        ).astype(jnp.float32),
    )
    blocks = jnp.arange(groups, dtype=jnp.int32)
    holder = jnp.sum((ends[None, :] <= blocks[:, None]).astype(jnp.int32), axis=1)
    wanted = holder * capacity + blocks - starts[holder]
    weights, first, second = tuple((jnp.take(item, wanted, axis=2) for item in arrived))
    half = weights.astype(jnp.bfloat16)
    gathered = lax.all_gather(inputs, "tensor", axis=2, tiled=True)
    tokens = gathered.reshape(-1, width)
    backs = cotangent.reshape(-1, width)
    whole = lax.all_gather(half, "dp", axis=0, tiled=True)
    gate = jnp.dot(tokens, whole[:, 0, :], preferred_element_type=jnp.float32)
    up = jnp.dot(tokens, whole[:, 1, :], preferred_element_type=jnp.float32)
    back = jnp.dot(backs, whole[:, 2, :], preferred_element_type=jnp.float32)
    act, slope = silu_parts(gate)
    hidden = (act * up).astype(jnp.bfloat16)
    dgate = (back * up * slope).astype(jnp.bfloat16)
    dup = (back * act).astype(jnp.bfloat16)
    grad = lax.psum_scatter(
        jnp.stack(
            [
                contract_rows(tokens, dgate),
                contract_rows(tokens, dup),
                contract_rows(backs, hidden),
            ],
            axis=1,
        ).astype(jnp.bfloat16),
        "dp",
        scatter_dimension=0,
        tiled=True,
    ).astype(jnp.float32)
    new_first = 0.9 * first + 0.1 * grad
    new_second = 0.95 * second + 0.05 * grad * grad
    new_weights = weights - 8e-05 * (new_first / (jnp.sqrt(new_second) + 1e-08) + 0.1 * weights)
    return (new_weights, new_first, new_second)


def solution(mesh):
    in_specs = (
        P(None, ("dp", "tensor"), None),
        P(None, ("dp", "tensor"), None),
        P(None, ("dp", "tensor"), None),
        P(),
        P(),
        P(None, "dp", "tensor"),
        P(None, "dp", None),
    )
    out_specs = (P("dp", None, "tensor"), P("dp", None, "tensor"), P("dp", None, "tensor"))
    return jax.shard_map(
        on_device, mesh=mesh, in_specs=in_specs, out_specs=out_specs, check_vma=False
    )
```

profile of v0, /device:TPU:0, one launch (start us, length us, event | category | flops | bytes accessed | tf_op | source)
XLA Modules:
  0.0 405.9 jit_solution(2938689487685794631)
XLA Ops:
  7.2 0.7 all-gather.5.cloned.1.call-update
  7.9 0.8 copy.40
  8.9 0.7 sub.12
  9.6 1.2 dynamic_slice.11
  10.9 0.6 dynamic_slice.9
  13.4 0.8 pad_dynamic-slice_fusion
  14.2 1.7 broadcast_in_dim.63
  16.0 1.8 broadcast_in_dim.66
  17.8 2.7 broadcast_in_dim.68
  20.5 0.7 iota_compare_fusion.2
  21.2 15.0 %select_reduce_fusion = (bf16[3,2,4,16384]{3,2,1,0:T(4,128)(2,1)}, bf16[3,2,4,16384]{3,2,1,0:T(4,128)(2,1)}, bf16[3,2,4,16384]{3,2,1,0:T(4,128)(2,1)}) fusion(f32[3,2,4,16384]{3,2,1,0:T(4,128)} %broadcast_in_dim.68, pred[2,4,4]{2,1,0:T(4,128)(4,1)S(1)} %fusion.17, f32[3,2,4,16384]{3,2,1,0:T(4,128)S(1)} %broadcast_in_dim.66, ...), kind=kLoop, calls=%fused_computation.11 | loop fusion | flops 8257536 | bytes 7077920 | tf_op jit(solution)/shard_map/reduce_sum | solution.py:38
  36.2 2.1 convert_element_type.65
  38.3 1.7 copy.54
  40.0 11.7 %all-to-all-start = ((bf16[512,3,256]{0,1,2:T(4,128)(2,1)}), bf16[512,3,256]{0,1,2:T(4,128)(2,1)}, u32[]{:S(2)}, u32[]{:S(2)}) async-start(bf16[512,3,256]{0,1,2:T(4,128)(2,1)} %bitcast.6), calls=%async_computation | async-start | bytes 2097152 | tf_op jit(solution)/shard_map/all_to_all | solution.py:46
  51.8 1.2 gather_fusion
  53.1 28.5 %all-to-all-done = bf16[512,3,256]{0,1,2:T(4,128)(2,1)} async-done(((bf16[512,3,256]{0,1,2:T(4,128)(2,1)}), bf16[512,3,256]{0,1,2:T(4,128)(2,1)}, u32[]{:S(2)}, u32[]{:S(2)}) %all-to-all-start) | async-done | bytes 786464 | tf_op jit(solution)/shard_map/all_to_all | solution.py:46
  81.7 1.5 convert_element_type.68
  83.2 1.2 gather_fusion.1
  84.4 1.1 bitcast_convert_fusion
  85.5 0.2 reduce-scatter.2.cloned.1.call-start
  85.7 82.8 %all-gather.5.cloned.1.call-done = bf16[2,240,16384]{2,1,0:T(8,128)(2,1)} async-done(((bf16[2,240,4096]{2,1,0:T(8,128)(2,1)}), bf16[2,240,16384]{2,1,0:T(8,128)(2,1)}) %all-gather.5.cloned.1.call-update) | async-done | bytes 15728656 | tf_op jit(solution)/shard_map/all_gather | solution.py:61
  168.6 74.1 %all-gather.3.cloned.1.call-done = bf16[16384,3,128]{0,2,1:T(8,128)(2,1)} async-done(((bf16[512,3,128]{0,2,1:T(8,128)(2,1)}), bf16[16384,3,128]{0,2,1:T(8,128)(2,1)}) %all-gather.3.cloned.1.call-update) | async-done | bytes 12582928 | tf_op jit(solution)/shard_map/all_gather | solution.py:64
  242.7 9.3 %fusion.8 = f32[480,128]{1,0:T(8,128)S(1)} fusion(bf16[480,16384]{1,0:T(8,128)(2,1)} %bitcast.74, bf16[16384,3,128]{0,2,1:T(8,128)(2,1)} %all-gather.3.cloned.1.call-done), kind=kOutput, calls=%fused_computation.23 | convolution fusion | flops 2013265920 | bytes 20168704 | tf_op jit(solution)/shard_map/dot_general | solution.py:65
  252.1 9.0 %fusion.6 = f32[480,128]{1,0:T(8,128)S(1)} fusion(bf16[480,16384]{1,0:T(8,128)(2,1)} %bitcast.80, bf16[16384,3,128]{0,2,1:T(8,128)(2,1)} %all-gather.3.cloned.1.call-done), kind=kOutput, calls=%fused_computation.21 | convolution fusion | flops 2013265920 | bytes 20168704 | tf_op jit(solution)/shard_map/dot_general | solution.py:67
  261.2 2.7 fusion.1
  263.9 7.1 %fusion.7 = f32[480,128]{1,0:T(8,128)} fusion(bf16[480,16384]{1,0:T(8,128)(2,1)S(1)} %bitcast.78, bf16[16384,3,128]{0,2,1:T(8,128)(2,1)} %all-gather.3.cloned.1.call-done), kind=kOutput, calls=%fused_computation.22 | convolution fusion | flops 2013265920 | bytes 20168704 | tf_op jit(solution)/shard_map/dot_general | solution.py:66
  270.9 4.0 fusion
  274.9 8.2 %fusion.2 = bf16[16384,1,128]{0,2,1:T(8,128)(2,1)S(1)} fusion(bf16[480,16384]{1,0:T(8,128)(2,1)} %bitcast.81, f32[480,128]{1,0:T(8,128)} %fusion.7, f32[480,128]{1,0:T(8,128)} %copy-done.2), kind=kOutput, calls=%fused_computation.9 | convolution fusion | flops 2015731712 | bytes 20414464 | tf_op jit(solution)/shard_map/dot_general | solution.py:13
  283.1 5.6 %pad_maximum_fusion = bf16[16384,3,128]{0,2,1:T(8,128)(2,1)} fusion(bf16[16384,1,128]{0,2,1:T(8,128)(2,1)S(1)} %fusion.2, bf16[16384,1,128]{0,2,1:T(8,128)(2,1)S(1)} %fusion.1, bf16[16384,1,128]{0,2,1:T(8,128)(2,1)S(1)} %fusion), kind=kLoop, calls=%fused_computation.10 | loop fusion | flops 12582912 | bytes 25165824 | tf_op jit(solution)/shard_map/stack | solution.py:73
  288.8 1.1 copy-done.4
  289.9 0.6 convert_element_type.71
  290.5 1.7 copy.55
  292.2 8.5 %all-to-all-start.1 = ((bf16[512,3,256]{0,1,2:T(4,128)(2,1)}), bf16[512,3,256]{0,1,2:T(4,128)(2,1)S(1)}, u32[]{:S(2)}, u32[]{:S(2)}) async-start(bf16[512,3,256]{0,1,2:T(4,128)(2,1)} %bitcast.9), calls=%async_computation.1 | async-start | bytes 2097152 | tf_op jit(solution)/shard_map/all_to_all | solution.py:49
  300.7 2.2 convert_element_type.81
  302.9 1.7 copy.56
  304.6 15.0 %all-to-all-done.1 = bf16[512,3,256]{0,1,2:T(4,128)(2,1)S(1)} async-done(((bf16[512,3,256]{0,1,2:T(4,128)(2,1)}), bf16[512,3,256]{0,1,2:T(4,128)(2,1)S(1)}, u32[]{:S(2)}, u32[]{:S(2)}) %all-to-all-start.1) | async-done | bytes 786464 | tf_op jit(solution)/shard_map/all_to_all | solution.py:49
  319.6 1.0 copy-done.3
  320.6 5.7 %all-to-all-start.2 = ((bf16[512,3,256]{0,1,2:T(4,128)(2,1)}), bf16[512,3,256]{0,1,2:T(4,128)(2,1)}, u32[]{:S(2)}, u32[]{:S(2)}) async-start(bf16[512,3,256]{0,1,2:T(4,128)(2,1)} %bitcast.26), calls=%async_computation.3 | async-start | bytes 2097152 | tf_op jit(solution)/shard_map/all_to_all | solution.py:52
  326.4 1.6 convert_element_type.74
  327.9 2.2 gather_fusion.2
  330.1 14.8 %all-to-all-done.2 = bf16[512,3,256]{0,1,2:T(4,128)(2,1)} async-done(((bf16[512,3,256]{0,1,2:T(4,128)(2,1)}), bf16[512,3,256]{0,1,2:T(4,128)(2,1)}, u32[]{:S(2)}, u32[]{:S(2)}) %all-to-all-start.2) | async-done | bytes 786464 | tf_op jit(solution)/shard_map/all_to_all | solution.py:52
  344.9 1.5 convert_element_type.84
  346.4 2.1 gather_fusion.3
  348.5 44.7 %reduce-scatter.2.cloned.1.call-done = bf16[512,3,128]{0,2,1:T(8,128)(2,1)} async-done(((bf16[16384,3,128]{0,2,1:T(8,128)(2,1)}), bf16[512,3,128]{0,2,1:T(8,128)(2,1)}) %reduce-scatter.2.cloned.1.call-update) | async-done | bytes 393232 | tf_op jit(solution)/shard_map/reduce_scatter | solution.py:72
  393.2 2.8 bitcast_subtract_fusion
  396.0 1.1 copy.51
  397.1 1.1 copy.52
  398.3 1.1 copy.53
  (32 shorter events, 0.7 us)
Async XLA Ops:
  7.2 161.4 %all-gather.5.cloned.1.call-start = ((), (), s32[]{:S(2)}) async-start(), calls=%async_computation.5 | async-start | bytes 19660800 | tf_op jit(solution)/shard_map/all_gather | solution.py:61
  40.0 41.7 %all-to-all-start = ((bf16[512,3,256]{0,1,2:T(4,128)(2,1)}), bf16[512,3,256]{0,1,2:T(4,128)(2,1)}, u32[]{:S(2)}, u32[]{:S(2)}) async-start(bf16[512,3,256]{0,1,2:T(4,128)(2,1)} %bitcast.6), calls=%async_computation | async-start | bytes 2097152 | tf_op jit(solution)/shard_map/all_to_all | solution.py:46
  51.7 191.0 %all-gather.3.cloned.1.call-start = ((), (), s32[]{:S(2)}) async-start(), calls=%async_computation.4 | async-start | bytes 12976128 | tf_op jit(solution)/shard_map/all_gather | solution.py:64
  84.4 167.7 %copy-start = (f32[128,512,3]{1,2,0:T(4,128)}, f32[128,512,3]{1,2,0:T(4,128)S(1)}, u32[]{:S(2)}) copy-start(f32[128,512,3]{1,2,0:T(4,128)S(1)} %gather_fusion.1) | copy-start | bytes 2359300
  85.5 307.7 %reduce-scatter.2.cloned.1.call-start = ((), (), s32[]{:S(2)}) async-start(), calls=%async_computation.6 | async-start | bytes 12976128 | tf_op jit(solution)/shard_map/reduce_scatter | solution.py:72
  242.7 18.4 %slice-start = ((s8[15728640]{0:T(1024)(128)(4,1)}), s8[4194304]{0:T(1024)(128)(4,1)S(1)}, s32[]{:S(2)}) async-start(s8[15728640]{0:T(1024)(128)(4,1)} %bitcast.75), calls=%async_computation.7 | async-start | bytes 8388608
  242.7 18.4 %slice-start.1 = ((s8[15728640]{0:T(1024)(128)(4,1)}), s8[4194304]{0:T(1024)(128)(4,1)S(1)}, s32[]{:S(2)}) async-start(s8[15728640]{0:T(1024)(128)(4,1)} %bitcast.75), calls=%async_computation.8 | async-start | bytes 8388608
  252.0 9.1 %copy-start.2 = (f32[480,128]{1,0:T(8,128)}, f32[480,128]{1,0:T(8,128)S(1)}, u32[]{:S(2)}) copy-start(f32[480,128]{1,0:T(8,128)S(1)} %fusion.8) | copy-start | bytes 737284
  252.0 9.1 %slice-start.2 = ((s8[15728640]{0:T(1024)(128)(4,1)}), s8[4194304]{0:T(1024)(128)(4,1)S(1)}, s32[]{:S(2)}) async-start(s8[15728640]{0:T(1024)(128)(4,1)} %bitcast.75), calls=%async_computation.9 | async-start | bytes 8388608
  252.0 9.1 %slice-start.3 = ((s8[15728640]{0:T(1024)(128)(4,1)}), s8[3145728]{0:T(1024)(128)(4,1)S(1)}, s32[]{:S(2)}) async-start(s8[15728640]{0:T(1024)(128)(4,1)} %bitcast.75), calls=%async_computation.10 | async-start | bytes 6291456
  261.2 2.7 copy-start.5
  288.7 1.1 copy-start.4
  292.2 27.4 %all-to-all-start.1 = ((bf16[512,3,256]{0,1,2:T(4,128)(2,1)}), bf16[512,3,256]{0,1,2:T(4,128)(2,1)S(1)}, u32[]{:S(2)}, u32[]{:S(2)}) async-start(bf16[512,3,256]{0,1,2:T(4,128)(2,1)} %bitcast.9), calls=%async_computation.1 | async-start | bytes 2097152 | tf_op jit(solution)/shard_map/all_to_all | solution.py:49
  300.6 92.5 %copy-start.1 = (f32[128,512,3]{1,2,0:T(4,128)S(1)}, f32[128,512,3]{1,2,0:T(4,128)}, u32[]{:S(2)}) copy-start(f32[128,512,3]{1,2,0:T(4,128)} %copy-done) | copy-start | bytes 2359300
  319.6 1.1 copy-start.3
  320.6 24.2 %all-to-all-start.2 = ((bf16[512,3,256]{0,1,2:T(4,128)(2,1)}), bf16[512,3,256]{0,1,2:T(4,128)(2,1)}, u32[]{:S(2)}, u32[]{:S(2)}) async-start(bf16[512,3,256]{0,1,2:T(4,128)(2,1)} %bitcast.26), calls=%async_computation.3 | async-start | bytes 2097152 | tf_op jit(solution)/shard_map/all_to_all | solution.py:52
Sparse Core Ops, SparseCore 0:
  9.7 158.8 all-gather.4
  171.3 71.3 all-gather.2
  288.9 104.2 reduce-scatter.1
where the time goes:
time: 407 us; the launch traced here: 406 us
  waiting for transfers between devices  261 us (64%)
  matrix products  40.3 us (10%)
  local copies, waits for them, and re-layouts  31.9 us (8%)
  other arithmetic  30.9 us (8%)
  starting transfers between devices  26.2 us (6%)
  between operations  16 us (4%)
    all_gather x1, waiting for transfers between devices, on_device(): gathered = lax.all_gather(inputs, 'tensor', axis=2, tiled=True)  82.8 us
    all_gather x1, waiting for transfers between devices, on_device(): whole = lax.all_gather(half, 'dp', axis=0, tiled=True)  74.1 us
    reduce_scatter x1, waiting for transfers between devices, on_device(): lax.psum_scatter(jnp.stack([contract_rows(tokens, dgate), contract_rows(t...  44.7 us
    all_to_all x1, waiting for transfers between devices, on_device(): lax.all_to_all(sent[0].astype(jnp.bfloat16), ('dp', 'tensor'), split_axis...  28.5 us
    all_to_all x1, waiting for transfers between devices, on_device(): lax.all_to_all(sent[1].astype(jnp.bfloat16), ('dp', 'tensor'), split_axis...  15 us
    reduce_sum x1, other arithmetic, outgoing(): jnp.sum(jnp.where(picked[None, :, :, :, None], pieces[:, :, None, :, :],...  15 us
    dot_general x3, matrix products, contract_rows(): lax.dot_general(left, right, (((0,), (0,)), ((), ())), preferred_element_...  14.8 us
    all_to_all x1, waiting for transfers between devices, on_device(): lax.all_to_all(sent[2].astype(jnp.bfloat16), ('dp', 'tensor'), split_axis...  14.8 us
  transfers between devices with their start and end apart: 6, of which 6 were waited for; matrix products, arithmetic and copies ran while one was open for 12% of the time, Pallas kernels for 0%

commit v1 on v0

v1 whole, which is shorter than its diff:
```python
import functools

import jax
import jax.numpy as jnp
from jax import lax
from jax.experimental import pallas as pl
from jax.experimental.pallas import tpu as pltpu
from jax.sharding import Mesh, PartitionSpec as P

BF = jnp.bfloat16
F32 = jnp.float32
MESH = pl.DeviceIdType.MESH
NS = 256


def dot_nt(a, b):
    return lax.dot_general(a, b, (((1,), (1,)), ((), ())), preferred_element_type=F32)


def dot(a, b):
    return jnp.dot(a, b, preferred_element_type=F32)


def iota(shape, dim):
    return lax.broadcasted_iota(jnp.int32, shape, dim)


def kernel(
    blocks, owners, old_w, old_f, old_s, tok_in, cot_in,
    out_w, out_f, out_s,
    stage, xs, xr, mom, yx, swp, fin, wall, tok, cot, part, part_in, sgr, grd, r1, r2, ysum, r3, r4, zed,
    sel_a, sel_b, perm, perm64, perm128,
    ssem, rsem, lsem,
):
    z, y, c, x = (lax.axis_index(a) for a in ("z", "y", "c", "x"))
    step4 = lambda v, d: lax.rem(v + d + 4, 4)
    counter = [0]
    started = []

    def copy(src, dst, dev):
        n = counter[0]
        counter[0] += 1
        d = pltpu.make_async_remote_copy(
            src_ref=src, dst_ref=dst, send_sem=ssem.at[n], recv_sem=rsem.at[n],
            device_id=dev, device_id_type=MESH,
        )
        d.start()
        started.append(d)
        return d

    barrier = pltpu.get_barrier_semaphore()

    def greet(dev):
        pl.semaphore_signal(barrier, inc=1, device_id=dev, device_id_type=MESH)

    for d in (1, 2, 3):
        greet({"x": step4(x, d)})
        greet({"y": step4(y, d)})
    for d in (1, 3):
        greet({"z": step4(z, d)})
    greet({"c": 1 - c})
    for zs in range(4):
        for cs in range(2):
            greet({"x": z, "z": zs, "c": cs})

    olds = (old_w, old_f, old_s)
    local = []

    def load(src, dst):
        d = pltpu.make_async_copy(src, dst, lsem.at[len(local)])
        d.start()
        local.append(d)
        return d

    loads = [load(olds[k // 3].at[k % 3], stage.at[k]) for k in range(9)]
    quarter = pl.ds(pl.multiple_of(x * 4096, 4096), 4096)
    tload = []
    for mb in range(2):
        rows = pl.ds(240 * mb, 240)
        tload.append(load(tok_in.at[rows], tok.at[2 * c + mb, pl.ds(0, 240)]))
        tload.append(load(cot_in.at[rows, quarter], cot.at[2 * c + mb, pl.ds(0, 240)]))
    tok[:, 240:, :] = jnp.zeros((4, 16, 4096), BF)
    cot[:, 240:, :] = jnp.zeros((4, 16, 4096), BF)

    shape = (16, 64)
    row, col = iota(shape, 0), iota(shape, 1)
    ru, ri = row // 4, row % 4
    cx, ch, cj, cs = col // 16, (col // 8) % 2, (col // 4) % 2, col % 4
    dp = z * 8 + y * 2 + c
    group = jnp.full(shape, -1, jnp.int32)
    for xx in range(4):
        held = blocks[dp * 4 + xx]
        base = 2 * (xx // 2) + (blocks[dp * 4 + xx - 1] if xx % 2 else 0)
        for j in range(2):
            group = jnp.where((cx == xx) & (cj == j), jnp.where(j < held, base + j, -1), group)
    who = jnp.full(shape, -1, jnp.int32)
    for i in range(4):
        for s in range(4):
            who = jnp.where((ri == i) & (cs == s), owners[s, dp * 4 + i], who)
    hit = (group == ri) & (who == ru)
    sel_a[...] = jnp.where(hit & (ch == 0), 1.0, 0.0).astype(BF)
    sel_b[...] = jnp.where(hit & (ch == 1), 1.0, 0.0).astype(BF)
    r, q = iota((64, 64), 0), iota((64, 64), 1)
    want = ((r // 4) % 4) * 16 + (r // 16) * 4 + r % 4
    perm64[...] = jnp.where(q == want, 1.0, 0.0).astype(BF)
    r, q = iota((256, 256), 0), iota((256, 256), 1)
    want = (r // 64) * 64 + ((r // 4) % 4) * 16 + ((r // 16) % 4) * 4 + r % 4
    perm[...] = jnp.where(q == want, 1.0, 0.0).astype(BF)
    r, q = iota((128, 128), 0), iota((128, 128), 1)
    want = (r // 32) * 32 + ((r // 4) % 2) * 16 + ((r // 8) % 4) * 4 + r % 4
    perm128[...] = jnp.where(q == want, 1.0, 0.0).astype(BF)

    def pack(k):
        loads[k].wait()
        for xx in range(4):
            lo = stage[k, :, xx * 4096 : xx * 4096 + 2048]
            hi = stage[k, :, xx * 4096 + 2048 : xx * 4096 + 4096]
            xs[k, xx] = jnp.concatenate([lo, hi], axis=0).astype(BF)
        xr[k, x] = xs[k, x]

    pack(0)
    pl.semaphore_wait(barrier, 17)

    xcop = {}

    def xsend(k, n):
        ks = pl.ds(k, n)
        for d in (1, 3, 2):
            xcop[k, d] = copy(xs.at[ks, step4(x, d)], xr.at[ks, x], {"x": step4(x, d)})

    xsend(0, 1)
    sib = {"c": 1 - c}
    mine = []
    for mb in range(2):
        rows = pl.ds(240 * mb, 240)
        mine.append(copy(tok_in.at[rows], tok.at[2 * c + mb, pl.ds(0, 240)], sib))
    pack(1)
    xsend(1, 1)
    pack(2)
    xsend(2, 1)
    mine_cot = []
    for mb in range(2):
        rows = pl.ds(240 * mb, 240)
        mine_cot.append(copy(cot_in.at[rows, quarter], cot.at[2 * c + mb, pl.ds(0, 240)], sib))

    def xwait(k):
        for d in (1, 3, 2):
            xcop[k, d].wait_recv()

    def select(k):
        rows = xr[k].reshape(64, 2048)
        return dot(sel_a[...], rows).astype(BF), dot(sel_b[...], rows).astype(BF)

    def wref(m, h, first, second, lo, n):
        cols = pl.ds(2048 * h + lo, n)
        if h == 0:
            return wall.at[m, second, first, :, cols]
        return wall.at[m, first, second, :, cols]

    def ring1(h, d):
        return {"y": step4(y, d)} if h == 0 else {"z": step4(z, d)}

    def ring2(h, d):
        return {"z": step4(z, d)} if h == 0 else {"y": step4(y, d)}

    def at1(h, d):
        return step4(y if h == 0 else z, d)

    def at2(h, d):
        return step4(z if h == 0 else y, d)

    ag = {}
    ITEM = (0, -1, 1, 2)

    def out2(m, h, j):
        piece = wref(m, h, at1(h, ITEM[j]), at2(h, 0), 0, 2048)
        ag[m, h, j, "l"] = copy(piece, piece, ring2(h, 1))
        ag[m, h, j, "r"] = copy(piece, piece, ring2(h, -1))

    def ag1(m):
        xwait(m)
        a, b = select(m)
        wall[m, z, y, :, 0:2048] = a
        wall[m, z, y, :, 2048:4096] = b
        for yy in range(4):
            half = a if yy < 2 else b
            mom[m, yy] = half[:, 1024 * (yy % 2) : 1024 * (yy % 2) + 1024]
        for h in range(2):
            piece = wref(m, h, at1(h, 0), at2(h, 0), 0, 2048)
            ag[m, h, "l"] = copy(piece, piece, ring1(h, 1))
            ag[m, h, "r"] = copy(piece, piece, ring1(h, -1))
        for h in range(2):
            out2(m, h, 0)

    def ag2(m):
        for h in range(2):
            ag[m, h, "l"].wait_recv()
            piece = wref(m, h, at1(h, -1), at2(h, 0), 0, 1024)
            ag[m, h, "fl"] = copy(piece, piece, ring1(h, 1))
            ag[m, h, "r"].wait_recv()
            piece = wref(m, h, at1(h, 1), at2(h, 0), 1024, 1024)
            ag[m, h, "fr"] = copy(piece, piece, ring1(h, -1))
        for h in range(2):
            out2(m, h, 1)
            out2(m, h, 2)

    def forward(m, h, j):
        ag[m, h, j, "l"].wait_recv()
        piece = wref(m, h, at1(h, ITEM[j]), at2(h, -1), 0, 1024)
        ag[m, h, j, "fl"] = copy(piece, piece, ring2(h, 1))
        ag[m, h, j, "r"].wait_recv()
        piece = wref(m, h, at1(h, ITEM[j]), at2(h, 1), 1024, 1024)
        ag[m, h, j, "fr"] = copy(piece, piece, ring2(h, -1))

    def ag3(m):
        for h in range(2):
            ag[m, h, "fl"].wait_recv()
            ag[m, h, "fr"].wait_recv()
            out2(m, h, 3)
        for h in range(2):
            forward(m, h, 0)

    def ag4(m):
        for h in range(2):
            forward(m, h, 1)
            forward(m, h, 2)

    def ag5(m):
        for h in range(2):
            forward(m, h, 3)

    def ag6(m):
        for h in range(2):
            for j in range(4):
                ag[m, h, j, "fl"].wait_recv()
                ag[m, h, j, "fr"].wait_recv()

    pc = {}

    def fwd(m):
        acts = cot if m == 2 else tok

        def body(b, carry):
            part[m, b] = dot_nt(acts[b], wall[m].reshape(256, 4096)).astype(BF)
            return carry

        lax.fori_loop(0, 4, body, 0)
        for d in (1, 3, 2):
            pc[m, d] = copy(part.at[m, step4(x, d)], part_in.at[m, d - 1], {"x": step4(x, d)})

    def summed(m):
        for d in (1, 3, 2):
            pc[m, d].wait_recv()
        total = part[m, x].astype(F32)
        for d in range(3):
            total = total + part_in[m, d].astype(F32)
        return total

    sc = {}

    def share(m, value):
        sgr[m, x] = dot_nt(perm[...], value.astype(BF)).astype(BF)
        for d in (1, 3, 2):
            sc[m, d] = copy(sgr.at[m, x], sgr.at[m, x], {"x": step4(x, d)})

    def bwd(m):
        acts = cot if m == 2 else tok
        for d in (1, 3, 2):
            sc[m, d].wait_recv()

        def body(n, carry):
            cols = pl.ds(pl.multiple_of(n * 512, 512), 512)
            left = jnp.concatenate([sgr[m, b] for b in range(4)], axis=1)
            right = acts[:, :, cols].reshape(1024, 512)
            res = dot(left, right).astype(BF).reshape(4, 64, 512)
            grd[m, lax.rem(n, 2), n // 2] = res
            return carry

        lax.fori_loop(0, 8, body, 0)

    rs = {}

    def gref(m, h, p, q):
        return (m, h, q, p) if h == 0 else (m, h, p, q)

    def rs1(m):
        for h in range(2):
            far = at2(h, 2)
            for half in range(2):
                if h == 0:
                    src = grd.at[m, h, pl.ds(2 * half, 2), far]
                else:
                    src = grd.at[m, h, far, pl.ds(2 * half, 2)]
                rs[m, h, 1, half] = copy(src, r1.at[m, h, half], ring2(h, 1 if half == 0 else -1))

    def rs2(m):
        for h in range(2):
            for half in range(2):
                rs[m, h, 1, half].wait_recv()
                to = 1 if half == 0 else -1
                p = at2(h, to)
                for k in range(2):
                    at = gref(m, h, p, 2 * half + k)
                    grd[at] = (grd[at].astype(F32) + r1[m, h, half, k].astype(F32)).astype(BF)
                src = grd.at[m, h, :, p] if h == 0 else grd.at[m, h, p]
                rs[m, h, 2, half] = copy(src, r2.at[m, h, half], ring2(h, to))

    def rs3(m):
        for h in range(2):
            rs[m, h, 2, 0].wait_recv()
            rs[m, h, 2, 1].wait_recv()
            for q in range(4):
                own = grd[gref(m, h, at2(h, 0), q)].astype(F32)
                ysum[m, h, q] = (
                    own + r2[m, h, 0, q].astype(F32) + r2[m, h, 1, q].astype(F32)
                ).astype(BF)
            for half in range(2):
                src = ysum.at[m, h, at1(h, 2), pl.ds(32 * half, 32)]
                rs[m, h, 3, half] = copy(src, r3.at[m, h, half], ring1(h, 1 if half == 0 else -1))

    def rs4(m):
        for h in range(2):
            for half in range(2):
                rs[m, h, 3, half].wait_recv()
                to = 1 if half == 0 else -1
                p = at1(h, to)
                rows = pl.ds(32 * half, 32)
                ysum[m, h, p, rows] = (
                    ysum[m, h, p, rows].astype(F32) + r3[m, h, half].astype(F32)
                ).astype(BF)
                rs[m, h, 4, half] = copy(ysum.at[m, h, p], r4.at[m, h, half], ring1(h, to))

    def deliver(base, ref_of, dst):
        n0 = counter[0]
        counter[0] += 8
        pending = []
        for u in range(4):
            for h in range(2):
                same = (x == z) & (x == u) & (c == h)
                remote = pltpu.make_async_remote_copy(
                    src_ref=ref_of(u, h), dst_ref=dst, send_sem=ssem.at[n0 + u * 2 + h],
                    recv_sem=rsem.at[n0], device_id={"x": u, "z": x, "c": h}, device_id_type=MESH,
                )
                pending.append((same, remote))

                @pl.when(jnp.logical_not(same))
                def _():
                    remote.start()

                @pl.when(same)
                def _():
                    pltpu.make_async_copy(ref_of(u, h), dst, rsem.at[n0]).start()

        return n0, pending

    late = []
    gsem = {}

    def rs5(m):
        for h in range(2):
            rs[m, h, 4, 0].wait_recv()
            rs[m, h, 4, 1].wait_recv()
            own = ysum[m, h, at1(h, 0)].astype(F32)
            zed[m, h] = (
                own + r4[m, h, 0].astype(F32) + r4[m, h, 1].astype(F32)
            ).astype(BF).reshape(4, 16, 512)
        n0, pending = deliver(
            9 + m, lambda u, h: zed.at[m, h, u], fin.at[9 + m, z * 2 + c]
        )
        gsem[m] = n0
        late.extend(pending)

    def landed(n0, k, n):
        whole = fin.at[pl.ds(k, n)]
        pltpu.make_async_copy(whole, whole, rsem.at[n0]).wait()

    yc = {}
    msem = {}

    def mom_pick(a):
        xwait(3 * a)
        for k in range(3 * a, 3 * a + 3):
            lo, hi = select(k)
            for yy in range(4):
                half = lo if yy < 2 else hi
                mom[k, yy] = half[:, 1024 * (yy % 2) : 1024 * (yy % 2) + 1024]

    def mom_y():
        yx[y] = mom[:, y]
        for d in (1, 3, 2):
            yc[d] = copy(mom.at[:, step4(y, d)], yx.at[y], {"y": step4(y, d)})

    def mom_swap():
        for d in (1, 3, 2):
            yc[d].wait_recv()
        for k in range(9):
            res = dot(perm64[...], yx[:, k].reshape(64, 1024)).astype(BF)
            for u in range(4):
                for h in range(2):
                    swp[k, u, h] = res[16 * u : 16 * u + 16, 512 * h : 512 * h + 512]
        n0, pending = deliver(0, lambda u, h: swp.at[:, u, h], fin.at[pl.ds(0, 9), z * 2 + c])
        msem[0] = n0
        late.extend(pending)

    def owned(k):
        return dot(perm128[...], fin[k].reshape(128, 512)).T

    def mom_land():
        landed(msem[0], 0, 9)
        for m in range(3):
            out_w[m] = owned(m)
            out_f[m] = owned(3 + m)
            out_s[m] = owned(6 + m)

    def update(m):
        landed(gsem[m], 9 + m, 1)
        grad = owned(9 + m)
        w = out_w[m]
        first = 0.9 * out_f[m] + 0.1 * grad
        second = 0.95 * out_s[m] + 0.05 * grad * grad
        out_f[m] = first
        out_s[m] = second
        out_w[m] = w - 8e-05 * (first / (jnp.sqrt(second) + 1e-08) + 0.1 * w)

    ag1(0)
    ag1(1)
    ag2(0)
    ag1(2)
    for k in (3, 4, 5):
        pack(k)
    xsend(3, 3)
    ag3(0)
    ag2(1)
    ag4(0)
    for k in (6, 7, 8):
        pack(k)
    xsend(6, 3)
    ag3(1)
    ag2(2)
    ag5(0)
    for d in tload[0::2]:
        d.wait()
    for d in mine:
        d.wait_recv()
    ag4(1)
    ag3(2)
    ag6(0)
    fwd(0)
    ag5(1)
    ag4(2)
    mom_pick(1)
    mom_pick(2)
    mom_y()
    ag6(1)
    fwd(1)
    ag5(2)
    gate = summed(0)
    up = summed(1)
    sig = 1.0 / (1.0 + jnp.exp(-gate))
    act = gate * sig
    share(2, act * up)
    for d in tload[1::2]:
        d.wait()
    for d in mine_cot:
        d.wait_recv()
    ag6(2)
    fwd(2)
    bwd(2)
    rs1(2)
    back = summed(2)
    share(0, back * up * (sig * (1.0 + gate * (1.0 - sig))))
    share(1, back * act)
    rs2(2)
    mom_swap()
    bwd(0)
    rs1(0)
    rs3(2)
    rs2(0)
    bwd(1)
    rs1(1)
    rs4(2)
    rs3(0)
    rs2(1)
    mom_land()
    rs5(2)
    rs4(0)
    rs3(1)
    rs5(0)
    update(2)
    rs4(1)
    update(0)
    rs5(1)
    update(1)
    for d in started:
        d.wait_send()
    for same, d in late:

        @pl.when(jnp.logical_not(same))
        def _():
            d.wait_send()


def on_device(old_weights, old_first, old_second, old_blocks, owner_map, inputs, cotangent):
    any_ = pl.BlockSpec(memory_space=pl.ANY)
    smem = pl.BlockSpec(memory_space=pltpu.SMEM)
    vmem = pl.BlockSpec(memory_space=pltpu.VMEM)
    V = pltpu.VMEM
    outs = pl.pallas_call(
        kernel,
        out_shape=[jax.ShapeDtypeStruct((3, 512, 128), F32)] * 3,
        in_specs=[smem, smem, any_, any_, any_, any_, any_],
        out_specs=[vmem] * 3,
        scratch_shapes=[
            V((9, 8, 16384), F32),
            V((9, 4, 16, 2048), BF),
            V((9, 4, 16, 2048), BF),
            V((9, 4, 16, 1024), BF),
            V((4, 9, 16, 1024), BF),
            V((9, 4, 2, 16, 512), BF),
            V((12, 8, 16, 512), BF),
            V((3, 4, 4, 16, 4096), BF),
            V((4, 256, 4096), BF),
            V((4, 256, 4096), BF),
            V((3, 4, 256, 256), BF),
            V((3, 3, 256, 256), BF),
            V((3, 4, 256, 256), BF),
            V((3, 2, 4, 4, 64, 512), BF),
            V((3, 2, 2, 2, 64, 512), BF),
            V((3, 2, 2, 4, 64, 512), BF),
            V((3, 2, 4, 64, 512), BF),
            V((3, 2, 2, 32, 512), BF),
            V((3, 2, 2, 64, 512), BF),
            V((3, 2, 4, 16, 512), BF),
            V((16, 64), BF),
            V((16, 64), BF),
            V((256, 256), BF),
            V((64, 64), BF),
            V((128, 128), BF),
            pltpu.SemaphoreType.DMA((NS,)),
            pltpu.SemaphoreType.DMA((NS,)),
            pltpu.SemaphoreType.DMA((16,)),
        ],
        compiler_params=pltpu.CompilerParams(
            collective_id=0, has_side_effects=True, vmem_limit_bytes=64 * 1024 * 1024
        ),
        name="restore_step",
    )(
        old_blocks, owner_map.T, old_weights, old_first, old_second,
        inputs.reshape(480, 4096), cotangent.reshape(480, 16384),
    )
    return tuple(jnp.transpose(o, (1, 0, 2)) for o in outs)


def solution(mesh):
    grid = Mesh(mesh.devices.reshape(4, 4, 2, 4), ("z", "y", "c", "x"))
    dp = ("z", "y", "c")
    shard = P(None, ("z", "y", "c", "x"), None)
    in_specs = (shard, shard, shard, P(), P(), P(None, dp, "x"), P(None, dp, None))
    out_specs = (P(dp, None, "x"),) * 3
    return jax.shard_map(
        on_device, mesh=grid, in_specs=in_specs, out_specs=out_specs, check_vma=False
    )
```

time: 407 us -> 143 us (0.35)
  waiting for transfers between devices: 261 us -> 0 us
  Pallas kernels: 0 us -> 136 us
  matrix products: 40.3 us -> 0 us
  other arithmetic: 30.9 us -> 0 us
  local copies, waits for them, and re-layouts: 31.9 us -> 3.95 us
  starting transfers between devices: 26.2 us -> 0 us
  between operations: 16 us -> 0.66 us
    all_gather x2 -> x0, waiting for transfers between devices: 157 us -> none  [the longest x1 82.8 us: on_device(): gathered = lax.all_gather(inputs, 'tensor', axis=2, tiled=True)]
    pallas_call x0 -> x1, Pallas kernels: none -> 136 us  [on_device(): pl.pallas_call(kernel, out_shape=[jax.ShapeDtypeStruct((3, 512, 128), F32...]
    all_to_all x3 -> x0, waiting for transfers between devices: 58.3 us -> none  [the longest x1 28.5 us: on_device(): lax.all_to_all(sent[0].astype(jnp.bfloat16), ('dp', 'tensor'), split_axis...]
    reduce_scatter x1 -> x0, waiting for transfers between devices: 44.7 us -> none  [on_device(): lax.psum_scatter(jnp.stack([contract_rows(tokens, dgate), contract_rows(t...]
    dot_general x6 -> x0, matrix products: 40.3 us -> none  [the longest x3 14.8 us: contract_rows(): lax.dot_general(left, right, (((0,), (0,)), ((), ())), preferred_element_...]
    all_to_all x3 -> x0, starting transfers between devices: 25.9 us -> none  [the longest x1 11.7 us: on_device(): lax.all_to_all(sent[0].astype(jnp.bfloat16), ('dp', 'tensor'), split_axis...]
    reduce_sum x2 -> x0, other arithmetic: 15.1 us -> none  [the longest x1 15 us: outgoing(): jnp.sum(jnp.where(picked[None, :, :, :, None], pieces[:, :, None, :, :],...]
    convert_element_type x6 -> x0, local copies, waits for them, and re-layouts: 9.96 us -> none  [the longest x2 3.9 us: on_device(): sent[2].astype(jnp.bfloat16)]
  transfers between devices with their start and end apart: 6 -> 0, of which waited for: 6 -> 0; matrix products, arithmetic and copies ran while one was open for 12% -> 0% of each run, Pallas kernels for 0% -> 0%
where the time goes in v1:
time: 143 us; the launch traced here: 140 us
  Pallas kernels  136 us (95%)
  local copies, waits for them, and re-layouts  3.95 us (3%)
    pallas_call x1, Pallas kernels, on_device(): pl.pallas_call(kernel, out_shape=[jax.ShapeDtypeStruct((3, 512, 128), F32...  136 us
    unnamed x7, local copies, waits for them, and re-layouts  3.95 us

profile of v1, /device:TPU:0, one launch (start us, length us, event | category | flops | bytes accessed | tf_op | source)
XLA Modules:
  0.0 140.3 jit_solution(13758698182928771355)
XLA Ops:
  0.6 135.7 %restore_step.1 = (f32[3,512,128]{2,1,0:T(8,128)}, f32[3,512,128]{2,1,0:T(8,128)}, f32[3,512,128]{2,1,0:T(8,128)}) custom-call(s32[128]{0:T(128)} %blocks.1, s32[4,128]{1,0:T(4,128)} %bitcast.11, f32[3,8,16384]{2,1,0:T(8,128)} %old_w.1, f32[3,8,16384]{2,1,0:T(8,128)} %old_f.1, f32[3,8,16384]{2,1,0:T(8,128)} %old_s.1, bf16[480,4096]{1,0:T(8,128)(2,1)} %bitcast.7, ...), custom_call_target="tpu_custom_call" | custom-call | tf_op jit(solution)/shard_map/restore_step/pallas_call | solution.py:508
  136.3 0.0 copy-start.1
  136.3 0.0 copy-start
  136.3 2.2 %copy.13 = f32[512,3,128]{2,0,1:T(8,128)} copy(f32[512,3,128]{2,0,1:T(8,128)} %bitcast.10) | data formatting | bytes 1572864
  138.5 0.0 copy-done.1
  138.5 0.9 copy.14
  139.4 0.0 copy-done
  139.4 0.9 copy.15
Async XLA Ops:
  136.3 2.2 %copy-start.1 = (f32[3,512,128]{2,1,0:T(8,128)S(1)}, f32[3,512,128]{2,1,0:T(8,128)}, u32[]{:S(2)}) copy-start(f32[3,512,128]{2,1,0:T(8,128)} %get-tuple-element.7) | copy-start | bytes 2359300
  136.3 3.1 %copy-start = (f32[3,512,128]{2,1,0:T(8,128)S(1)}, f32[3,512,128]{2,1,0:T(8,128)}, u32[]{:S(2)}) copy-start(f32[3,512,128]{2,1,0:T(8,128)} %get-tuple-element.8) | copy-start | bytes 2359300

commit v2 on v1

v2 whole, which is shorter than its diff:
```python
import functools

import jax
import jax.numpy as jnp
from jax import lax
from jax.experimental import pallas as pl
from jax.experimental.pallas import tpu as pltpu
from jax.sharding import Mesh, PartitionSpec as P

BF = jnp.bfloat16
F32 = jnp.float32
MESH = pl.DeviceIdType.MESH
NS = 320


def dot_nt(a, b):
    return lax.dot_general(a, b, (((1,), (1,)), ((), ())), preferred_element_type=F32)


def dot(a, b):
    return jnp.dot(a, b, preferred_element_type=F32)


def iota(shape, dim):
    return lax.broadcasted_iota(jnp.int32, shape, dim)


def kernel(
    blocks, owners, old_w, old_f, old_s, tok_in, cot_in,
    out,
    stage, xs, xr, mom, yx, swp, fin, wall, tok, cot, part, part_in, sgr, grd, r1, r2, ysum, r4, zed,
    sel_a, sel_b, perm, perm64, perm128,
    ssem, rsem, lsem, gsum,
):
    z, y, c, x = (lax.axis_index(a) for a in ("z", "y", "c", "x"))
    step4 = lambda v, d: lax.rem(v + d + 4, 4)
    counter = [0]
    started = []

    def copy(src, dst, dev):
        n = counter[0]
        counter[0] += 1
        d = pltpu.make_async_remote_copy(
            src_ref=src, dst_ref=dst, send_sem=ssem.at[n], recv_sem=rsem.at[n],
            device_id=dev, device_id_type=MESH,
        )
        d.start()
        started.append(d)
        return d

    barrier = pltpu.get_barrier_semaphore()

    def greet(dev):
        pl.semaphore_signal(barrier, inc=1, device_id=dev, device_id_type=MESH)

    for d in (1, 2, 3):
        greet({"x": step4(x, d)})
        greet({"y": step4(y, d)})
    for d in (1, 3):
        greet({"z": step4(z, d)})
    greet({"c": 1 - c})
    for zs in range(4):
        for cs in range(2):
            greet({"x": z, "z": zs, "c": cs})

    olds = (old_w, old_f, old_s)
    local = []

    def load(src, dst):
        d = pltpu.make_async_copy(src, dst, lsem.at[len(local)])
        d.start()
        local.append(d)
        return d

    loads = [load(olds[k // 3].at[k % 3], stage.at[k]) for k in range(9)]
    quarter = pl.ds(pl.multiple_of(x * 4096, 4096), 4096)
    tload = []
    for mb in range(2):
        rows = pl.ds(240 * mb, 240)
        tload.append(load(tok_in.at[rows], tok.at[2 * c + mb, pl.ds(0, 240)]))
        tload.append(load(cot_in.at[rows, quarter], cot.at[2 * c + mb, pl.ds(0, 240)]))
    tok[:, 240:, :] = jnp.zeros((4, 16, 4096), BF)
    cot[:, 240:, :] = jnp.zeros((4, 16, 4096), BF)

    shape = (16, 64)
    row, col = iota(shape, 0), iota(shape, 1)
    ru, ri = row // 4, row % 4
    cx, ch, cj, cs = col // 16, (col // 8) % 2, (col // 4) % 2, col % 4
    dp = z * 8 + y * 2 + c
    group = jnp.full(shape, -1, jnp.int32)
    for xx in range(4):
        held = blocks[dp * 4 + xx]
        base = 2 * (xx // 2) + (blocks[dp * 4 + xx - 1] if xx % 2 else 0)
        for j in range(2):
            group = jnp.where((cx == xx) & (cj == j), jnp.where(j < held, base + j, -1), group)
    who = jnp.full(shape, -1, jnp.int32)
    for i in range(4):
        for s in range(4):
            who = jnp.where((ri == i) & (cs == s), owners[s, dp * 4 + i], who)
    hit = (group == ri) & (who == ru)
    sel_a[...] = jnp.where(hit & (ch == 0), 1.0, 0.0).astype(BF)
    sel_b[...] = jnp.where(hit & (ch == 1), 1.0, 0.0).astype(BF)
    r, q = iota((64, 64), 0), iota((64, 64), 1)
    want = ((r // 4) % 4) * 16 + (r // 16) * 4 + r % 4
    perm64[...] = jnp.where(q == want, 1.0, 0.0).astype(BF)
    r, q = iota((256, 256), 0), iota((256, 256), 1)
    want = (r // 64) * 64 + ((r // 4) % 4) * 16 + ((r // 16) % 4) * 4 + r % 4
    perm[...] = jnp.where(q == want, 1.0, 0.0).astype(BF)
    r, q = iota((128, 128), 0), iota((128, 128), 1)
    want = (r // 32) * 32 + ((r // 4) % 2) * 16 + ((r // 8) % 4) * 4 + r % 4
    perm128[...] = jnp.where(q == want, 1.0, 0.0).astype(BF)

    def pack(k):
        loads[k].wait()
        for xx in range(4):
            lo = stage[k, :, xx * 4096 : xx * 4096 + 2048]
            hi = stage[k, :, xx * 4096 + 2048 : xx * 4096 + 4096]
            xs[k, xx] = jnp.concatenate([lo, hi], axis=0).astype(BF)
        xr[k, x] = xs[k, x]

    pack(0)
    pl.semaphore_wait(barrier, 17)

    xcop = {}

    def xsend(k, n):
        ks = pl.ds(k, n)
        for d in (1, 3, 2):
            xcop[k, d] = copy(xs.at[ks, step4(x, d)], xr.at[ks, x], {"x": step4(x, d)})

    xsend(0, 1)
    sib = {"c": 1 - c}
    mine, mine_cot = [], []
    for mb in range(2):
        rows = pl.ds(240 * mb, 240)
        mine.append(copy(tok_in.at[rows], tok.at[2 * c + mb, pl.ds(0, 240)], sib))
    for mb in range(2):
        rows = pl.ds(240 * mb, 240)
        mine_cot.append(copy(cot_in.at[rows, quarter], cot.at[2 * c + mb, pl.ds(0, 240)], sib))

    def xwait(k):
        for d in (1, 3, 2):
            xcop[k, d].wait_recv()

    def select(k):
        rows = xr[k].reshape(64, 2048)
        return dot(sel_a[...], rows).astype(BF), dot(sel_b[...], rows).astype(BF)

    def wref(m, h, first, second, lo, n):
        cols = pl.ds(2048 * h + lo, n)
        if h == 0:
            return wall.at[m, second, first, :, cols]
        return wall.at[m, first, second, :, cols]

    def ring1(h, d):
        return {"y": step4(y, d)} if h == 0 else {"z": step4(z, d)}

    def ring2(h, d):
        return {"z": step4(z, d)} if h == 0 else {"y": step4(y, d)}

    def at1(h, d):
        return step4(y if h == 0 else z, d)

    def at2(h, d):
        return step4(z if h == 0 else y, d)

    ag = {}
    ITEM = (0, -1, 1, 2)

    def out2(m, h, j):
        piece = wref(m, h, at1(h, ITEM[j]), at2(h, 0), 0, 2048)
        ag[m, h, j, "l"] = copy(piece, piece, ring2(h, 1))
        ag[m, h, j, "r"] = copy(piece, piece, ring2(h, -1))

    def pack_w(m):
        pack(m)
        xsend(m, 1)

    def ag1(m):
        xwait(m)
        a, b = select(m)
        wall[m, z, y, :, 0:2048] = a
        wall[m, z, y, :, 2048:4096] = b
        for h in range(2):
            piece = wref(m, h, at1(h, 0), at2(h, 0), 0, 2048)
            ag[m, h, "l"] = copy(piece, piece, ring1(h, 1))
            ag[m, h, "r"] = copy(piece, piece, ring1(h, -1))
        for h in range(2):
            out2(m, h, 0)

    def ag2(m, h, j):
        if j == 1:
            ag[m, h, "l"].wait_recv()
            piece = wref(m, h, at1(h, -1), at2(h, 0), 0, 1024)
            ag[m, h, "fl"] = copy(piece, piece, ring1(h, 1))
        elif j == 2:
            ag[m, h, "r"].wait_recv()
            piece = wref(m, h, at1(h, 1), at2(h, 0), 1024, 1024)
            ag[m, h, "fr"] = copy(piece, piece, ring1(h, -1))
        else:
            ag[m, h, "fl"].wait_recv()
            ag[m, h, "fr"].wait_recv()
        out2(m, h, j)

    def fw(m, h, j):
        ag[m, h, j, "l"].wait_recv()
        piece = wref(m, h, at1(h, ITEM[j]), at2(h, -1), 0, 1024)
        ag[m, h, j, "fl"] = copy(piece, piece, ring2(h, 1))
        ag[m, h, j, "r"].wait_recv()
        piece = wref(m, h, at1(h, ITEM[j]), at2(h, 1), 1024, 1024)
        ag[m, h, j, "fr"] = copy(piece, piece, ring2(h, -1))

    pc = {}
    ready = set()

    def acts_of(m):
        n = 1 if m == 2 else 0
        if n not in ready:
            ready.add(n)
            for d in tload[n::2]:
                d.wait()
            for d in (mine, mine_cot)[n]:
                d.wait_recv()
        return (tok, cot)[n]

    def fwd(m):
        acts = acts_of(m)
        for h in range(2):
            for j in range(4):
                ag[m, h, j, "fl"].wait_recv()
                ag[m, h, j, "fr"].wait_recv()

        def body(b, carry):
            part[m, b] = dot_nt(acts[b], wall[m].reshape(256, 4096)).astype(BF)
            return carry

        lax.fori_loop(0, 4, body, 0)
        rows = pl.ds(0, 240)
        for d in (1, 3, 2):
            pc[m, d] = copy(
                part.at[m, step4(x, d), rows], part_in.at[m, d - 1, rows], {"x": step4(x, d)}
            )

    def summed(m):
        for d in (1, 3, 2):
            pc[m, d].wait_recv()
        total = part[m, x].astype(F32)
        for d in range(3):
            total = total + part_in[m, d].astype(F32)
        return total

    sc = {}

    def share(m, value):
        sgr[m, x] = dot_nt(perm[...], value.astype(BF)).astype(BF)
        for d in (1, 3, 2):
            sc[m, d] = copy(sgr.at[m, x], sgr.at[m, x], {"x": step4(x, d)})

    kept = {}

    def hid():
        gate = summed(0)
        up = summed(1)
        sig = 1.0 / (1.0 + jnp.exp(-gate))
        act = gate * sig
        kept["act"] = act
        kept["slope"] = up * (sig * (1.0 + gate * (1.0 - sig)))
        share(2, act * up)

    def dg(m):
        if "back" not in kept:
            kept["back"] = summed(2)
        share(m, kept["back"] * kept["slope" if m == 0 else "act"])

    rs = {}

    def bwd(m):
        acts = acts_of(m)
        for d in (1, 3, 2):
            sc[m, d].wait_recv()

        def body(n, carry):
            cols = pl.ds(pl.multiple_of(n * 512, 512), 512)
            left = jnp.concatenate([sgr[m, b] for b in range(4)], axis=1)
            right = acts[:, :, cols].reshape(1024, 512)
            res = dot(left, right).astype(BF).reshape(4, 64, 512)
            grd[m, lax.rem(n, 2), n // 2] = res
            return carry

        lax.fori_loop(0, 8, body, 0)
        for h in range(2):
            far = at2(h, 2)
            for half in range(2):
                if h == 0:
                    src = grd.at[m, h, pl.ds(2 * half, 2), far]
                else:
                    src = grd.at[m, h, far, pl.ds(2 * half, 2)]
                rs[m, h, 1, half] = copy(src, r1.at[m, h, half], ring2(h, 1 if half == 0 else -1))

    def gref(m, h, p, q):
        return (m, h, q, p) if h == 0 else (m, h, p, q)

    def rs2(m, h):
        for half in range(2):
            rs[m, h, 1, half].wait_recv()
            to = 1 if half == 0 else -1
            p = at2(h, to)
            for k in range(2):
                at = gref(m, h, p, 2 * half + k)
                grd[at] = (grd[at].astype(F32) + r1[m, h, half, k].astype(F32)).astype(BF)
            src = grd.at[m, h, :, p] if h == 0 else grd.at[m, h, p]
            rs[m, h, 2, half] = copy(src, r2.at[m, h, half], ring2(h, to))

    def rs3(m, h):
        rs[m, h, 2, 0].wait_recv()
        rs[m, h, 2, 1].wait_recv()
        for q in range(4):
            own = grd[gref(m, h, at2(h, 0), q)].astype(F32)
            ysum[m, h, q] = (
                own + r2[m, h, 0, q].astype(F32) + r2[m, h, 1, q].astype(F32)
            ).astype(BF)
        for d in (2, 1, 3):
            rs[m, h, 4, d] = copy(ysum.at[m, h, at1(h, d)], r4.at[m, h, d - 1], ring1(h, d))

    def deliver(ref_of, dst):
        n0 = counter[0]
        counter[0] += 8
        for u in range(4):
            for h in range(2):
                same = (x == z) & (x == u) & (c == h)
                remote = pltpu.make_async_remote_copy(
                    src_ref=ref_of(u, h), dst_ref=dst, send_sem=ssem.at[n0 + u * 2 + h],
                    recv_sem=rsem.at[n0], device_id={"x": u, "z": x, "c": h}, device_id_type=MESH,
                )
                late.append((same, remote))

                @pl.when(jnp.logical_not(same))
                def _():
                    remote.start()

                @pl.when(same)
                def _():
                    pltpu.make_async_copy(ref_of(u, h), dst, rsem.at[n0]).start()

        return n0

    late = []
    gsem = {}
    msem = {}

    def rs5(m, h):
        for d in (1, 3, 2):
            rs[m, h, 4, d].wait_recv()
        own = ysum[m, h, at1(h, 0)].astype(F32)
        for d in range(3):
            own = own + r4[m, h, d].astype(F32)
        zed[m, h] = own.astype(BF).reshape(4, 16, 512)
        n0 = counter[0]
        counter[0] += 4
        gsem.setdefault(m, {})[h] = n0
        for u in range(4):
            same = (x == z) & (x == u) & (c == h)
            src, dst = zed.at[m, h, u], fin.at[9 + m, z * 2 + c]
            remote = pltpu.make_async_remote_copy(
                src_ref=src, dst_ref=dst, send_sem=ssem.at[n0 + u],
                recv_sem=gsum.at[m], device_id={"x": u, "z": x, "c": h}, device_id_type=MESH,
            )
            late.append((same, remote))

            @pl.when(jnp.logical_not(same))
            def _():
                remote.start()

            @pl.when(same)
            def _():
                pltpu.make_async_copy(src, dst, gsum.at[m]).start()

    def landed(sem, k, n):
        whole = fin.at[pl.ds(k, n)]
        pltpu.make_async_copy(whole, whole, sem).wait()

    yc = {}

    def mpack(a):
        for k in range(3 * a, 3 * a + 3):
            pack(k)
        xsend(3 * a, 3)

    def mpick(a):
        xwait(3 * a)
        ks = pl.ds(3 * a, 3)
        for k in range(3 * a, 3 * a + 3):
            lo, hi = select(k)
            for yy in range(4):
                half = lo if yy < 2 else hi
                mom[k, yy] = half[:, 1024 * (yy % 2) : 1024 * (yy % 2) + 1024]
        yx[y, ks] = mom[ks, y]
        for d in (1, 3, 2):
            yc[a, d] = copy(mom.at[ks, step4(y, d)], yx.at[y, ks], {"y": step4(y, d)})

    def mswap(a):
        if a:
            for d in (1, 3, 2):
                yc[a, d].wait_recv()
        for k in range(3 * a, 3 * a + 3):
            if a:
                rows = yx[:, k].reshape(64, 1024)
            else:
                cols = pl.ds(pl.multiple_of(y * 1024, 1024), 1024)
                rows = wall[k, z, :, :, cols].reshape(64, 1024)
            res = dot(perm64[...], rows).astype(BF)
            for u in range(4):
                for h in range(2):
                    swp[k, u, h] = res[16 * u : 16 * u + 16, 512 * h : 512 * h + 512]
        ks = pl.ds(3 * a, 3)
        msem[a] = deliver(lambda u, h: swp.at[ks, u, h], fin.at[ks, z * 2 + c])

    def owned(k):
        out[k] = dot(perm128[...], fin[k].reshape(128, 512)).T.astype(BF)

    def mland(a):
        landed(rsem.at[msem[a]], 3 * a, 3)
        for k in range(3 * a, 3 * a + 3):
            owned(k)

    def upd(m):
        landed(gsum.at[m], 9 + m, 1)
        owned(9 + m)

    part_in[:, :, 240:, :] = jnp.zeros((3, 3, 16, 256), BF)
    pack_w(1)
    ag1(0)
    mpack(2)
    ag1(1)
    ag2(1, 0, 1)
    ag2(1, 0, 2)
    ag2(1, 1, 2)
    ag2(1, 1, 1)
    pack_w(2)
    ag2(0, 1, 1)
    fw(1, 0, 0)
    ag2(0, 0, 1)
    ag2(0, 0, 2)
    ag2(1, 1, 3)
    fw(1, 0, 2)
    ag2(1, 0, 3)
    fw(1, 1, 1)
    mpack(1)
    fw(0, 1, 1)
    fw(1, 1, 3)
    fw(1, 1, 0)
    ag2(0, 1, 2)
    fw(1, 1, 2)
    ag2(0, 0, 3)
    fw(1, 0, 3)
    fw(1, 0, 1)
    fw(0, 0, 2)
    fw(0, 0, 0)
    ag2(0, 1, 3)
    fw(0, 0, 1)
    fw(0, 1, 0)
    ag1(2)
    fwd(1)
    fw(0, 0, 3)
    fw(0, 1, 2)
    fw(0, 1, 3)
    ag2(2, 0, 1)
    ag2(2, 0, 2)
    ag2(2, 1, 2)
    mpick(2)
    ag2(2, 1, 1)
    fwd(0)
    fw(2, 1, 0)
    fw(2, 0, 1)
    fw(2, 0, 0)
    ag2(2, 1, 3)
    ag2(2, 0, 3)
    mswap(2)
    fw(2, 1, 3)
    fw(2, 0, 3)
    hid()
    fw(2, 1, 1)
    fw(2, 1, 2)
    fw(2, 0, 2)
    fwd(2)
    mswap(0)
    mpick(1)
    bwd(2)
    dg(1)
    rs2(2, 0)
    rs2(2, 1)
    dg(0)
    mswap(1)
    bwd(1)
    rs3(2, 0)
    mland(2)
    rs3(2, 1)
    bwd(0)
    rs2(1, 1)
    rs2(1, 0)
    mland(1)
    rs5(2, 1)
    mland(0)
    rs5(2, 0)
    rs2(0, 1)
    rs2(0, 0)
    rs3(1, 0)
    rs3(1, 1)
    rs3(0, 1)
    rs3(0, 0)
    rs5(1, 0)
    upd(2)
    rs5(1, 1)
    rs5(0, 0)
    rs5(0, 1)
    upd(1)
    upd(0)
    for d in started:
        d.wait_send()
    for same, d in late:

        @pl.when(jnp.logical_not(same))
        def _():
            d.wait_send()


def on_device(old_weights, old_first, old_second, old_blocks, owner_map, inputs, cotangent):
    any_ = pl.BlockSpec(memory_space=pl.ANY)
    smem = pl.BlockSpec(memory_space=pltpu.SMEM)
    vmem = pl.BlockSpec(memory_space=pltpu.VMEM)
    V = pltpu.VMEM
    states = pl.pallas_call(
        kernel,
        out_shape=jax.ShapeDtypeStruct((12, 512, 128), BF),
        in_specs=[smem, smem, any_, any_, any_, any_, any_],
        out_specs=vmem,
        scratch_shapes=[
            V((9, 8, 16384), F32),
            V((9, 4, 16, 2048), BF),
            V((9, 4, 16, 2048), BF),
            V((9, 4, 16, 1024), BF),
            V((4, 9, 16, 1024), BF),
            V((9, 4, 2, 16, 512), BF),
            V((12, 8, 16, 512), BF),
            V((3, 4, 4, 16, 4096), BF),
            V((4, 256, 4096), BF),
            V((4, 256, 4096), BF),
            V((3, 4, 256, 256), BF),
            V((3, 3, 256, 256), BF),
            V((3, 4, 256, 256), BF),
            V((3, 2, 4, 4, 64, 512), BF),
            V((3, 2, 2, 2, 64, 512), BF),
            V((3, 2, 2, 4, 64, 512), BF),
            V((3, 2, 4, 64, 512), BF),
            V((3, 2, 3, 64, 512), BF),
            V((3, 2, 4, 16, 512), BF),
            V((16, 64), BF),
            V((16, 64), BF),
            V((256, 256), BF),
            V((64, 64), BF),
            V((128, 128), BF),
            pltpu.SemaphoreType.DMA((NS,)),
            pltpu.SemaphoreType.DMA((NS,)),
            pltpu.SemaphoreType.DMA((16,)),
            pltpu.SemaphoreType.DMA((3,)),
        ],
        compiler_params=pltpu.CompilerParams(
            collective_id=0, has_side_effects=True, vmem_limit_bytes=64 * 1024 * 1024
        ),
        name="restore_step",
    )(
        old_blocks, owner_map.T, old_weights, old_first, old_second,
        inputs.reshape(480, 4096), cotangent.reshape(480, 16384),
    )
    w, first, second, grad = (states[3 * i : 3 * i + 3].astype(F32) for i in range(4))
    first = 0.9 * first + 0.1 * grad
    second = 0.95 * second + 0.05 * grad * grad
    w = w - 8e-05 * (first / (jnp.sqrt(second) + 1e-08) + 0.1 * w)
    return tuple(jnp.transpose(o, (1, 0, 2)) for o in (w, first, second))


def solution(mesh):
    grid = Mesh(mesh.devices.reshape(4, 4, 2, 4), ("z", "y", "c", "x"))
    dp = ("z", "y", "c")
    shard = P(None, ("z", "y", "c", "x"), None)
    in_specs = (shard, shard, shard, P(), P(), P(None, dp, "x"), P(None, dp, None))
    out_specs = (P(dp, None, "x"),) * 3
    return jax.shard_map(
        on_device, mesh=grid, in_specs=in_specs, out_specs=out_specs, check_vma=False
    )
```

time: 143 us -> 133 us (0.930); the launches traced: 140 us -> 132 us
  Pallas kernels: 136 us -> 128 us
  local copies, waits for them, and re-layouts: 3.95 us -> 0 us
  other arithmetic: 0 us -> 3.15 us
    pallas_call x1, Pallas kernels: 136 us -> 128 us  [on_device(): pl.pallas_call(kernel, out_shape=jax.ShapeDtypeStruct((12, 512, 128), BF)...]
    unnamed x7 -> x0, local copies, waits for them, and re-layouts: 3.95 us -> none
    transpose x0 -> x1, other arithmetic: none -> 3.15 us  [on_device(): return tuple((jnp.transpose(o, (1, 0, 2)) for o in (w, first, second)))]
where the time goes in v2:
time: 133 us; the launch traced here: 132 us
  Pallas kernels  128 us (96%)
  other arithmetic  3.15 us (2%)
    pallas_call x1, Pallas kernels, on_device(): pl.pallas_call(kernel, out_shape=jax.ShapeDtypeStruct((12, 512, 128), BF)...  128 us
    transpose x1, other arithmetic, on_device(): return tuple((jnp.transpose(o, (1, 0, 2)) for o in (w, first, second)))  3.15 us

profile of v2, /device:TPU:0, one launch (start us, length us, event | category | flops | bytes accessed | tf_op | source)
XLA Modules:
  0.0 131.8 jit_solution(4660375217239236415)
XLA Ops:
  0.6 128.0 %restore_step.1 = bf16[12,512,128]{2,1,0:T(8,128)(2,1)} custom-call(s32[128]{0:T(128)} %blocks.1, s32[4,128]{1,0:T(4,128)} %bitcast.11, f32[3,8,16384]{2,1,0:T(8,128)} %old_w.1, f32[3,8,16384]{2,1,0:T(8,128)} %old_f.1, f32[3,8,16384]{2,1,0:T(8,128)} %old_s.1, bf16[480,4096]{1,0:T(8,128)(2,1)} %bitcast.10, bf16[480,16384]{1,0:T(8,128)(2,1)} %bitcast.9), custom_call_target="tpu_custom_call" | custom-call | tf_op jit(solution)/shard_map/restore_step/pallas_call | solution.py:532
  128.6 3.1 %fusion.6 = (f32[512,3,128]{2,0,1:T(8,128)}, f32[512,3,128]{2,0,1:T(8,128)}, f32[512,3,128]{2,0,1:T(8,128)}) fusion(bf16[12,512,128]{2,1,0:T(8,128)(2,1)} %restore_step.1), kind=kLoop, calls=%fused_computation.10 | loop fusion | flops 3342336 | bytes 3932160 | tf_op jit(solution)/shard_map/transpose | solution.py:579

commit v3 on v2

--- a/solution.py
+++ b/solution.py
@@ -10,7 +10,7 @@
 BF = jnp.bfloat16
 F32 = jnp.float32
 MESH = pl.DeviceIdType.MESH
-NS = 320
+NS = 400
 
 
 def dot_nt(a, b):
@@ -186,20 +186,13 @@
             ag[m, h, "l"] = copy(piece, piece, ring1(h, 1))
             ag[m, h, "r"] = copy(piece, piece, ring1(h, -1))
         for h in range(2):
+            piece = wref(m, h, at1(h, 0), at2(h, 0), 0, 2048)
+            ag[m, h, "o"] = copy(piece, piece, ring1(h, 2))
+        for h in range(2):
             out2(m, h, 0)
 
     def ag2(m, h, j):
-        if j == 1:
-            ag[m, h, "l"].wait_recv()
-            piece = wref(m, h, at1(h, -1), at2(h, 0), 0, 1024)
-            ag[m, h, "fl"] = copy(piece, piece, ring1(h, 1))
-        elif j == 2:
-            ag[m, h, "r"].wait_recv()
-            piece = wref(m, h, at1(h, 1), at2(h, 0), 1024, 1024)
-            ag[m, h, "fr"] = copy(piece, piece, ring1(h, -1))
-        else:
-            ag[m, h, "fl"].wait_recv()
-            ag[m, h, "fr"].wait_recv()
+        ag[m, h, (None, "l", "r", "o")[j]].wait_recv()
         out2(m, h, j)
 
     def fw(m, h, j):
@@ -230,16 +223,32 @@
                 ag[m, h, j, "fl"].wait_recv()
                 ag[m, h, j, "fr"].wait_recv()
 
-        def body(b, carry):
+        n0 = counter[0]
+        counter[0] += 3
+        rows = pl.ds(0, 240)
+
+        def piece(d, n):
+            b = step4(x, d)
+            return pltpu.make_async_remote_copy(
+                src_ref=part.at[m, b, rows], dst_ref=part_in.at[m, d - 1, rows],
+                send_sem=ssem.at[n], recv_sem=rsem.at[n],
+                device_id={"x": b}, device_id_type=MESH,
+            )
+
+        def body(i, carry):
+            b = step4(x, i + 1)
             part[m, b] = dot_nt(acts[b], wall[m].reshape(256, 4096)).astype(BF)
+
+            @pl.when(i < 3)
+            def _():
+                piece(i + 1, n0 + i).start()
+
             return carry
 
         lax.fori_loop(0, 4, body, 0)
-        rows = pl.ds(0, 240)
-        for d in (1, 3, 2):
-            pc[m, d] = copy(
-                part.at[m, step4(x, d), rows], part_in.at[m, d - 1, rows], {"x": step4(x, d)}
-            )
+        for d in (1, 2, 3):
+            pc[m, d] = piece(d, n0 + d - 1)
+            started.append(pc[m, d])
 
     def summed(m):
         for d in (1, 3, 2):
@@ -381,47 +390,40 @@
 
     yc = {}
 
-    def mpack(a):
-        for k in range(3 * a, 3 * a + 3):
-            pack(k)
-        xsend(3 * a, 3)
-
-    def mpick(a):
-        xwait(3 * a)
-        ks = pl.ds(3 * a, 3)
-        for k in range(3 * a, 3 * a + 3):
-            lo, hi = select(k)
-            for yy in range(4):
-                half = lo if yy < 2 else hi
-                mom[k, yy] = half[:, 1024 * (yy % 2) : 1024 * (yy % 2) + 1024]
-        yx[y, ks] = mom[ks, y]
+    def mpack(k):
+        pack(k)
+        xsend(k, 1)
+
+    def mpick(k):
+        xwait(k)
+        lo, hi = select(k)
+        for yy in range(4):
+            half = lo if yy < 2 else hi
+            mom[k, yy] = half[:, 1024 * (yy % 2) : 1024 * (yy % 2) + 1024]
+        yx[k, y] = mom[k, y]
         for d in (1, 3, 2):
-            yc[a, d] = copy(mom.at[ks, step4(y, d)], yx.at[y, ks], {"y": step4(y, d)})
-
-    def mswap(a):
-        if a:
+            yc[k, d] = copy(mom.at[k, step4(y, d)], yx.at[k, y], {"y": step4(y, d)})
+
+    def mswap(k):
+        if k > 2:
             for d in (1, 3, 2):
-                yc[a, d].wait_recv()
-        for k in range(3 * a, 3 * a + 3):
-            if a:
-                rows = yx[:, k].reshape(64, 1024)
-            else:
-                cols = pl.ds(pl.multiple_of(y * 1024, 1024), 1024)
-                rows = wall[k, z, :, :, cols].reshape(64, 1024)
-            res = dot(perm64[...], rows).astype(BF)
-            for u in range(4):
-                for h in range(2):
-                    swp[k, u, h] = res[16 * u : 16 * u + 16, 512 * h : 512 * h + 512]
-        ks = pl.ds(3 * a, 3)
-        msem[a] = deliver(lambda u, h: swp.at[ks, u, h], fin.at[ks, z * 2 + c])
+                yc[k, d].wait_recv()
+            rows = yx[k].reshape(64, 1024)
+        else:
+            cols = pl.ds(pl.multiple_of(y * 1024, 1024), 1024)
+            rows = wall[k, z, :, :, cols].reshape(64, 1024)
+        res = dot(perm64[...], rows).astype(BF)
+        for u in range(4):
+            for h in range(2):
+                swp[k, u, h] = res[16 * u : 16 * u + 16, 512 * h : 512 * h + 512]
+        msem[k] = deliver(lambda u, h: swp.at[k, u, h], fin.at[k, z * 2 + c])
 
     def owned(k):
         out[k] = dot(perm128[...], fin[k].reshape(128, 512)).T.astype(BF)
 
-    def mland(a):
-        landed(rsem.at[msem[a]], 3 * a, 3)
-        for k in range(3 * a, 3 * a + 3):
-            owned(k)
+    def mland(k):
+        landed(rsem.at[msem[k]], k, 1)
+        owned(k)
 
     def upd(m):
         landed(gsum.at[m], 9 + m, 1)
@@ -429,90 +431,110 @@
 
     part_in[:, :, 240:, :] = jnp.zeros((3, 3, 16, 256), BF)
     pack_w(1)
+    mpack(4)
+    mpack(6)
+    mpack(5)
     ag1(0)
-    mpack(2)
     ag1(1)
+    ag2(1, 0, 2)
+    ag2(1, 1, 1)
+    ag2(1, 0, 3)
+    ag2(0, 1, 1)
+    ag2(1, 1, 3)
+    mpack(3)
     ag2(1, 0, 1)
-    ag2(1, 0, 2)
     ag2(1, 1, 2)
-    ag2(1, 1, 1)
+    ag2(0, 1, 2)
+    ag2(0, 1, 3)
     pack_w(2)
-    ag2(0, 1, 1)
+    ag2(0, 0, 2)
+    ag2(0, 0, 3)
+    ag2(0, 0, 1)
+    fw(1, 0, 3)
+    fw(1, 1, 0)
+    fw(1, 1, 1)
+    fw(1, 0, 2)
+    mpack(7)
+    fw(1, 1, 3)
+    fw(1, 0, 1)
+    fw(1, 1, 2)
     fw(1, 0, 0)
-    ag2(0, 0, 1)
-    ag2(0, 0, 2)
-    ag2(1, 1, 3)
-    fw(1, 0, 2)
-    ag2(1, 0, 3)
-    fw(1, 1, 1)
-    mpack(1)
+    fw(0, 1, 0)
+    fw(0, 1, 3)
+    fw(0, 0, 3)
     fw(0, 1, 1)
-    fw(1, 1, 3)
-    fw(1, 1, 0)
-    ag2(0, 1, 2)
-    fw(1, 1, 2)
-    ag2(0, 0, 3)
-    fw(1, 0, 3)
-    fw(1, 0, 1)
+    fw(0, 0, 0)
+    fw(0, 1, 2)
     fw(0, 0, 2)
-    fw(0, 0, 0)
-    ag2(0, 1, 3)
     fw(0, 0, 1)
-    fw(0, 1, 0)
     ag1(2)
+    mpack(8)
     fwd(1)
-    fw(0, 0, 3)
-    fw(0, 1, 2)
-    fw(0, 1, 3)
+    mpick(5)
     ag2(2, 0, 1)
+    mpick(8)
+    fwd(0)
+    ag2(2, 1, 2)
+    ag2(2, 1, 1)
+    ag2(2, 1, 3)
     ag2(2, 0, 2)
-    ag2(2, 1, 2)
-    mpick(2)
-    ag2(2, 1, 1)
-    fwd(0)
-    fw(2, 1, 0)
+    ag2(2, 0, 3)
+    mswap(0)
+    mpick(6)
+    fw(2, 0, 2)
+    fw(2, 1, 1)
     fw(2, 0, 1)
     fw(2, 0, 0)
-    ag2(2, 1, 3)
-    ag2(2, 0, 3)
+    fw(2, 1, 2)
+    fw(2, 1, 0)
+    mswap(5)
+    fw(2, 0, 3)
+    fw(2, 1, 3)
+    hid()
+    fwd(2)
+    mswap(1)
+    mswap(8)
+    mland(5)
+    bwd(2)
     mswap(2)
-    fw(2, 1, 3)
-    fw(2, 0, 3)
-    hid()
-    fw(2, 1, 1)
-    fw(2, 1, 2)
-    fw(2, 0, 2)
-    fwd(2)
-    mswap(0)
-    mpick(1)
-    bwd(2)
     dg(1)
+    dg(0)
+    mpick(7)
+    mswap(6)
     rs2(2, 0)
+    mpick(4)
+    mpick(3)
+    mland(1)
     rs2(2, 1)
-    dg(0)
-    mswap(1)
+    mswap(4)
+    mswap(7)
     bwd(1)
     rs3(2, 0)
-    mland(2)
     rs3(2, 1)
     bwd(0)
     rs2(1, 1)
     rs2(1, 0)
-    mland(1)
-    rs5(2, 1)
-    mland(0)
-    rs5(2, 0)
     rs2(0, 1)
     rs2(0, 0)
     rs3(1, 0)
+    rs5(2, 0)
+    mland(2)
     rs3(1, 1)
     rs3(0, 1)
     rs3(0, 0)
+    mland(4)
+    rs5(2, 1)
+    mswap(3)
+    rs5(1, 1)
     rs5(1, 0)
+    mland(0)
+    mland(8)
+    mland(6)
+    mland(7)
+    rs5(0, 1)
+    rs5(0, 0)
     upd(2)
-    rs5(1, 1)
-    rs5(0, 0)
-    rs5(0, 1)
+    mland(3)
     upd(1)
     upd(0)
     for d in started:
@@ -539,7 +561,7 @@
             V((9, 4, 16, 2048), BF),
             V((9, 4, 16, 2048), BF),
             V((9, 4, 16, 1024), BF),
-            V((4, 9, 16, 1024), BF),
+            V((9, 4, 16, 1024), BF),
             V((9, 4, 2, 16, 512), BF),
             V((12, 8, 16, 512), BF),
             V((3, 4, 4, 16, 4096), BF),

time: 133 us -> 129 us (0.970)
  Pallas kernels: 128 us -> 124 us
    pallas_call x1, Pallas kernels: 128 us -> 124 us  [on_device(): pl.pallas_call(kernel, out_shape=jax.ShapeDtypeStruct((12, 512, 128), BF)...]
where the time goes in v3:
time: 129 us; the launch traced here: 128 us
  Pallas kernels  124 us (96%)
  other arithmetic  3.15 us (2%)
    pallas_call x1, Pallas kernels, on_device(): pl.pallas_call(kernel, out_shape=jax.ShapeDtypeStruct((12, 512, 128), BF)...  124 us
    transpose x1, other arithmetic, on_device(): return tuple((jnp.transpose(o, (1, 0, 2)) for o in (w, first, second)))  3.15 us

profile of v3, /device:TPU:0, one launch (start us, length us, event | category | flops | bytes accessed | tf_op | source)
XLA Modules:
  0.0 128.2 jit_solution(13664611464201932223)
XLA Ops:
  0.6 124.4 %restore_step.1 = bf16[12,512,128]{2,1,0:T(8,128)(2,1)} custom-call(s32[128]{0:T(128)} %blocks.1, s32[4,128]{1,0:T(4,128)} %bitcast.11, f32[3,8,16384]{2,1,0:T(8,128)} %old_w.1, f32[3,8,16384]{2,1,0:T(8,128)} %old_f.1, f32[3,8,16384]{2,1,0:T(8,128)} %old_s.1, bf16[480,4096]{1,0:T(8,128)(2,1)} %bitcast.10, bf16[480,16384]{1,0:T(8,128)(2,1)} %bitcast.9), custom_call_target="tpu_custom_call" | custom-call | tf_op jit(solution)/shard_map/restore_step/pallas_call | solution.py:554
  125.0 3.1 %fusion.6 = (f32[512,3,128]{2,0,1:T(8,128)}, f32[512,3,128]{2,0,1:T(8,128)}, f32[512,3,128]{2,0,1:T(8,128)}) fusion(bf16[12,512,128]{2,1,0:T(8,128)(2,1)} %restore_step.1), kind=kLoop, calls=%fused_computation.10 | loop fusion | flops 3342336 | bytes 3932160 | tf_op jit(solution)/shard_map/transpose | solution.py:601

commit v4 on v3

--- a/solution.py
+++ b/solution.py
@@ -10,7 +10,7 @@
 BF = jnp.bfloat16
 F32 = jnp.float32
 MESH = pl.DeviceIdType.MESH
-NS = 400
+NS = 98
 
 
 def dot_nt(a, b):
@@ -30,23 +30,27 @@
     out,
     stage, xs, xr, mom, yx, swp, fin, wall, tok, cot, part, part_in, sgr, grd, r1, r2, ysum, r4, zed,
     sel_a, sel_b, perm, perm64, perm128,
-    ssem, rsem, lsem, gsum,
+    ssem, rsem, lsem,
 ):
     z, y, c, x = (lax.axis_index(a) for a in ("z", "y", "c", "x"))
     step4 = lambda v, d: lax.rem(v + d + 4, 4)
-    counter = [0]
-    started = []
-
-    def copy(src, dst, dev):
-        n = counter[0]
-        counter[0] += 1
-        d = pltpu.make_async_remote_copy(
-            src_ref=src, dst_ref=dst, send_sem=ssem.at[n], recv_sem=rsem.at[n],
-            device_id=dev, device_id_type=MESH,
-        )
-        d.start()
-        started.append(d)
-        return d
+    received = {}
+    SENT = ("gather", "x", "part", "share", "y", "r1", "r2", "r4", "sib", "hop")
+
+    def sem(*name):
+        return rsem.at[received.setdefault(name, len(received))]
+
+    def copy(src, dst, dev, kind, *name):
+        pltpu.make_async_remote_copy(
+            src_ref=src, dst_ref=dst, send_sem=ssem.at[SENT.index(kind)],
+            recv_sem=sem(kind, *name), device_id=dev, device_id_type=MESH,
+        ).start()
+
+    def arrived(like, kind, *name):
+        pltpu.make_async_copy(like, like, sem(kind, *name)).wait()
+
+    def left(like, kind):
+        pltpu.make_async_copy(like, like, ssem.at[SENT.index(kind)]).wait()
 
     barrier = pltpu.get_barrier_semaphore()
 
@@ -121,26 +125,22 @@
     pack(0)
     pl.semaphore_wait(barrier, 17)
 
-    xcop = {}
-
     def xsend(k, n):
         ks = pl.ds(k, n)
         for d in (1, 3, 2):
-            xcop[k, d] = copy(xs.at[ks, step4(x, d)], xr.at[ks, x], {"x": step4(x, d)})
+            copy(xs.at[ks, step4(x, d)], xr.at[ks, x], {"x": step4(x, d)}, "x", k)
 
     xsend(0, 1)
     sib = {"c": 1 - c}
-    mine, mine_cot = [], []
     for mb in range(2):
         rows = pl.ds(240 * mb, 240)
-        mine.append(copy(tok_in.at[rows], tok.at[2 * c + mb, pl.ds(0, 240)], sib))
+        copy(tok_in.at[rows], tok.at[2 * c + mb, pl.ds(0, 240)], sib, "sib", 0)
     for mb in range(2):
         rows = pl.ds(240 * mb, 240)
-        mine_cot.append(copy(cot_in.at[rows, quarter], cot.at[2 * c + mb, pl.ds(0, 240)], sib))
+        copy(cot_in.at[rows, quarter], cot.at[2 * c + mb, pl.ds(0, 240)], sib, "sib", 1)
 
     def xwait(k):
-        for d in (1, 3, 2):
-            xcop[k, d].wait_recv()
+        arrived(xr.at[k, pl.ds(0, 3)], "x", k)
 
     def select(k):
         rows = xr[k].reshape(64, 2048)
@@ -164,13 +164,12 @@
     def at2(h, d):
         return step4(z if h == 0 else y, d)
 
-    ag = {}
     ITEM = (0, -1, 1, 2)
 
     def out2(m, h, j):
         piece = wref(m, h, at1(h, ITEM[j]), at2(h, 0), 0, 2048)
-        ag[m, h, j, "l"] = copy(piece, piece, ring2(h, 1))
-        ag[m, h, j, "r"] = copy(piece, piece, ring2(h, -1))
+        for d in (1, -1):
+            copy(piece, piece, ring2(h, d), "gather", m, h, j)
 
     def pack_w(m):
         pack(m)
@@ -183,27 +182,24 @@
         wall[m, z, y, :, 2048:4096] = b
         for h in range(2):
             piece = wref(m, h, at1(h, 0), at2(h, 0), 0, 2048)
-            ag[m, h, "l"] = copy(piece, piece, ring1(h, 1))
-            ag[m, h, "r"] = copy(piece, piece, ring1(h, -1))
+            copy(piece, piece, ring1(h, 1), "gather", m, h, "l")
+            copy(piece, piece, ring1(h, -1), "gather", m, h, "r")
         for h in range(2):
             piece = wref(m, h, at1(h, 0), at2(h, 0), 0, 2048)
-            ag[m, h, "o"] = copy(piece, piece, ring1(h, 2))
+            copy(piece, piece, ring1(h, 2), "gather", m, h, "o")
         for h in range(2):
             out2(m, h, 0)
 
     def ag2(m, h, j):
-        ag[m, h, (None, "l", "r", "o")[j]].wait_recv()
+        arrived(wref(m, h, 0, 0, 0, 2048), "gather", m, h, (None, "l", "r", "o")[j])
         out2(m, h, j)
 
     def fw(m, h, j):
-        ag[m, h, j, "l"].wait_recv()
-        piece = wref(m, h, at1(h, ITEM[j]), at2(h, -1), 0, 1024)
-        ag[m, h, j, "fl"] = copy(piece, piece, ring2(h, 1))
-        ag[m, h, j, "r"].wait_recv()
-        piece = wref(m, h, at1(h, ITEM[j]), at2(h, 1), 1024, 1024)
-        ag[m, h, j, "fr"] = copy(piece, piece, ring2(h, -1))
-
-    pc = {}
+        arrived(wall.at[m, 0, pl.ds(0, 2), :, pl.ds(0, 2048)], "gather", m, h, j)
+        for lo, d in ((0, 1), (1024, -1)):
+            piece = wref(m, h, at1(h, ITEM[j]), at2(h, -d), lo, 1024)
+            copy(piece, piece, ring2(h, d), "gather", m)
+
     ready = set()
 
     def acts_of(m):
@@ -212,28 +208,14 @@
             ready.add(n)
             for d in tload[n::2]:
                 d.wait()
-            for d in (mine, mine_cot)[n]:
-                d.wait_recv()
+            arrived((tok, cot)[n].at[pl.ds(0, 2), pl.ds(0, 240)], "sib", n)
         return (tok, cot)[n]
 
     def fwd(m):
         acts = acts_of(m)
-        for h in range(2):
-            for j in range(4):
-                ag[m, h, j, "fl"].wait_recv()
-                ag[m, h, j, "fr"].wait_recv()
-
-        n0 = counter[0]
-        counter[0] += 3
+        arrived(wall.at[m, pl.ds(0, 2), :, :, pl.ds(0, 2048)], "gather", m)
+
         rows = pl.ds(0, 240)
-
-        def piece(d, n):
-            b = step4(x, d)
-            return pltpu.make_async_remote_copy(
-                src_ref=part.at[m, b, rows], dst_ref=part_in.at[m, d - 1, rows],
-                send_sem=ssem.at[n], recv_sem=rsem.at[n],
-                device_id={"x": b}, device_id_type=MESH,
-            )
 
         def body(i, carry):
             b = step4(x, i + 1)
@@ -241,29 +223,24 @@
 
             @pl.when(i < 3)
             def _():
-                piece(i + 1, n0 + i).start()
+                copy(part.at[m, b, rows], part_in.at[m, i, rows], {"x": b}, "part", m)
 
             return carry
 
         lax.fori_loop(0, 4, body, 0)
-        for d in (1, 2, 3):
-            pc[m, d] = piece(d, n0 + d - 1)
-            started.append(pc[m, d])
 
     def summed(m):
-        for d in (1, 3, 2):
-            pc[m, d].wait_recv()
+        arrived(part_in.at[m, :, pl.ds(0, 240)], "part", m)
         total = part[m, x].astype(F32)
         for d in range(3):
             total = total + part_in[m, d].astype(F32)
         return total
 
-    sc = {}
 
     def share(m, value):
         sgr[m, x] = dot_nt(perm[...], value.astype(BF)).astype(BF)
         for d in (1, 3, 2):
-            sc[m, d] = copy(sgr.at[m, x], sgr.at[m, x], {"x": step4(x, d)})
+            copy(sgr.at[m, x], sgr.at[m, x], {"x": step4(x, d)}, "share", m)
 
     kept = {}
 
@@ -281,12 +258,10 @@
             kept["back"] = summed(2)
         share(m, kept["back"] * kept["slope" if m == 0 else "act"])
 
-    rs = {}
 
     def bwd(m):
         acts = acts_of(m)
-        for d in (1, 3, 2):
-            sc[m, d].wait_recv()
+        arrived(sgr.at[m, pl.ds(0, 3)], "share", m)
 
         def body(n, carry):
             cols = pl.ds(pl.multiple_of(n * 512, 512), 512)
@@ -304,91 +279,56 @@
                     src = grd.at[m, h, pl.ds(2 * half, 2), far]
                 else:
                     src = grd.at[m, h, far, pl.ds(2 * half, 2)]
-                rs[m, h, 1, half] = copy(src, r1.at[m, h, half], ring2(h, 1 if half == 0 else -1))
+                copy(src, r1.at[m, h, half], ring2(h, 1 if half == 0 else -1), "r1", m, h)
 
     def gref(m, h, p, q):
         return (m, h, q, p) if h == 0 else (m, h, p, q)
 
     def rs2(m, h):
+        arrived(r1.at[m, h], "r1", m, h)
         for half in range(2):
-            rs[m, h, 1, half].wait_recv()
             to = 1 if half == 0 else -1
             p = at2(h, to)
             for k in range(2):
                 at = gref(m, h, p, 2 * half + k)
                 grd[at] = (grd[at].astype(F32) + r1[m, h, half, k].astype(F32)).astype(BF)
             src = grd.at[m, h, :, p] if h == 0 else grd.at[m, h, p]
-            rs[m, h, 2, half] = copy(src, r2.at[m, h, half], ring2(h, to))
+            copy(src, r2.at[m, h, half], ring2(h, to), "r2", m, h)
 
     def rs3(m, h):
-        rs[m, h, 2, 0].wait_recv()
-        rs[m, h, 2, 1].wait_recv()
+        arrived(r2.at[m, h], "r2", m, h)
         for q in range(4):
             own = grd[gref(m, h, at2(h, 0), q)].astype(F32)
             ysum[m, h, q] = (
                 own + r2[m, h, 0, q].astype(F32) + r2[m, h, 1, q].astype(F32)
             ).astype(BF)
         for d in (2, 1, 3):
-            rs[m, h, 4, d] = copy(ysum.at[m, h, at1(h, d)], r4.at[m, h, d - 1], ring1(h, d))
-
-    def deliver(ref_of, dst):
-        n0 = counter[0]
-        counter[0] += 8
-        for u in range(4):
-            for h in range(2):
-                same = (x == z) & (x == u) & (c == h)
-                remote = pltpu.make_async_remote_copy(
-                    src_ref=ref_of(u, h), dst_ref=dst, send_sem=ssem.at[n0 + u * 2 + h],
-                    recv_sem=rsem.at[n0], device_id={"x": u, "z": x, "c": h}, device_id_type=MESH,
-                )
-                late.append((same, remote))
-
-                @pl.when(jnp.logical_not(same))
-                def _():
-                    remote.start()
-
-                @pl.when(same)
-                def _():
-                    pltpu.make_async_copy(ref_of(u, h), dst, rsem.at[n0]).start()
-
-        return n0
-
-    late = []
-    gsem = {}
-    msem = {}
+            copy(ysum.at[m, h, at1(h, d)], r4.at[m, h, d - 1], ring1(h, d), "r4", m, h)
+
+    def deliver(src, u, h, k):
+        same = (x == z) & (x == u) & (c == h)
+        dst = fin.at[k, z * 2 + c]
+
+        @pl.when(jnp.logical_not(same))
+        def _():
+            copy(src, dst, {"x": u, "z": x, "c": h}, "hop", k)
+
+        @pl.when(same)
+        def _():
+            pltpu.make_async_copy(src, dst, sem("hop", k)).start()
 
     def rs5(m, h):
-        for d in (1, 3, 2):
-            rs[m, h, 4, d].wait_recv()
+        arrived(r4.at[m, h], "r4", m, h)
         own = ysum[m, h, at1(h, 0)].astype(F32)
         for d in range(3):
             own = own + r4[m, h, d].astype(F32)
         zed[m, h] = own.astype(BF).reshape(4, 16, 512)
-        n0 = counter[0]
-        counter[0] += 4
-        gsem.setdefault(m, {})[h] = n0
         for u in range(4):
-            same = (x == z) & (x == u) & (c == h)
-            src, dst = zed.at[m, h, u], fin.at[9 + m, z * 2 + c]
-            remote = pltpu.make_async_remote_copy(
-                src_ref=src, dst_ref=dst, send_sem=ssem.at[n0 + u],
-                recv_sem=gsum.at[m], device_id={"x": u, "z": x, "c": h}, device_id_type=MESH,
-            )
-            late.append((same, remote))
-
-            @pl.when(jnp.logical_not(same))
-            def _():
-                remote.start()
-
-            @pl.when(same)
-            def _():
-                pltpu.make_async_copy(src, dst, gsum.at[m]).start()
-
-    def landed(sem, k, n):
-        whole = fin.at[pl.ds(k, n)]
-        pltpu.make_async_copy(whole, whole, sem).wait()
-
-    yc = {}
+            deliver(zed.at[m, h, u], u, h, 9 + m)
+
+    def landed(k):
+        arrived(fin.at[k], "hop", k)
+
 
     def mpack(k):
         pack(k)
@@ -402,12 +342,11 @@
             mom[k, yy] = half[:, 1024 * (yy % 2) : 1024 * (yy % 2) + 1024]
         yx[k, y] = mom[k, y]
         for d in (1, 3, 2):
-            yc[k, d] = copy(mom.at[k, step4(y, d)], yx.at[k, y], {"y": step4(y, d)})
+            copy(mom.at[k, step4(y, d)], yx.at[k, y], {"y": step4(y, d)}, "y", k)
 
     def mswap(k):
         if k > 2:
-            for d in (1, 3, 2):
-                yc[k, d].wait_recv()
+            arrived(yx.at[k, pl.ds(0, 3)], "y", k)
             rows = yx[k].reshape(64, 1024)
         else:
             cols = pl.ds(pl.multiple_of(y * 1024, 1024), 1024)
@@ -416,17 +355,17 @@
         for u in range(4):
             for h in range(2):
                 swp[k, u, h] = res[16 * u : 16 * u + 16, 512 * h : 512 * h + 512]
-        msem[k] = deliver(lambda u, h: swp.at[k, u, h], fin.at[k, z * 2 + c])
+                deliver(swp.at[k, u, h], u, h, k)
 
     def owned(k):
         out[k] = dot(perm128[...], fin[k].reshape(128, 512)).T.astype(BF)
 
     def mland(k):
-        landed(rsem.at[msem[k]], k, 1)
+        landed(k)
         owned(k)
 
     def upd(m):
-        landed(gsum.at[m], 9 + m, 1)
+        landed(9 + m)
         owned(9 + m)
 
     part_in[:, :, 240:, :] = jnp.zeros((3, 3, 16, 256), BF)
@@ -537,13 +476,25 @@
     mland(3)
     upd(1)
     upd(0)
-    for d in started:
-        d.wait_send()
-    for same, d in late:
-
-        @pl.when(jnp.logical_not(same))
-        def _():
-            d.wait_send()
+    left(tok.at[pl.ds(0, 3), pl.ds(0, 240)], "gather")
+    left(xs.at[:, pl.ds(0, 3)], "x")
+    left(part_in.at[:, :, pl.ds(0, 240)], "part")
+    left(part_in, "share")
+    left(yx.at[pl.ds(0, 6), pl.ds(0, 3)], "y")
+    left(r1, "r1")
+    left(r2, "r2")
+    left(r4, "r4")
+    left(tok.at[:, pl.ds(0, 240)], "sib")
+
+    @pl.when(x == z)
+    def _():
+        left(fin.at[:, pl.ds(0, 7)], "hop")
+
+    @pl.when(x != z)
+    def _():
+        left(fin, "hop")
+
+    assert len(received) == NS, len(received)
 
 
 def on_device(old_weights, old_first, old_second, old_blocks, owner_map, inputs, cotangent):
@@ -581,10 +532,9 @@
             V((256, 256), BF),
             V((64, 64), BF),
             V((128, 128), BF),
+            pltpu.SemaphoreType.DMA((10,)),
             pltpu.SemaphoreType.DMA((NS,)),
-            pltpu.SemaphoreType.DMA((NS,)),
-            pltpu.SemaphoreType.DMA((16,)),
-            pltpu.SemaphoreType.DMA((3,)),
+            pltpu.SemaphoreType.DMA((13,)),
         ],
         compiler_params=pltpu.CompilerParams(
             collective_id=0, has_side_effects=True, vmem_limit_bytes=64 * 1024 * 1024

time: 129 us -> 122 us (0.946)
  Pallas kernels: 124 us -> 118 us
    pallas_call x1, Pallas kernels: 124 us -> 118 us  [on_device(): pl.pallas_call(kernel, out_shape=jax.ShapeDtypeStruct((12, 512, 128), BF)...]
where the time goes in v4:
time: 122 us
  Pallas kernels  118 us (97%)
  other arithmetic  3.15 us (3%)
    pallas_call x1, Pallas kernels, on_device(): pl.pallas_call(kernel, out_shape=jax.ShapeDtypeStruct((12, 512, 128), BF)...  118 us
    transpose x1, other arithmetic, on_device(): return tuple((jnp.transpose(o, (1, 0, 2)) for o in (w, first, second)))  3.15 us

profile of v4, /device:TPU:0, one launch (start us, length us, event | category | flops | bytes accessed | tf_op | source)
XLA Modules:
  0.0 121.7 jit_solution(16199449933500053110)
XLA Ops:
  0.6 117.9 %restore_step.1 = bf16[12,512,128]{2,1,0:T(8,128)(2,1)} custom-call(s32[128]{0:T(128)} %blocks.1, s32[4,128]{1,0:T(4,128)} %bitcast.11, f32[3,8,16384]{2,1,0:T(8,128)} %old_w.1, f32[3,8,16384]{2,1,0:T(8,128)} %old_f.1, f32[3,8,16384]{2,1,0:T(8,128)} %old_s.1, bf16[480,4096]{1,0:T(8,128)(2,1)} %bitcast.10, bf16[480,16384]{1,0:T(8,128)(2,1)} %bitcast.9), custom_call_target="tpu_custom_call" | custom-call | tf_op jit(solution)/shard_map/restore_step/pallas_call | solution.py:505
  118.6 3.1 %fusion.6 = (f32[512,3,128]{2,0,1:T(8,128)}, f32[512,3,128]{2,0,1:T(8,128)}, f32[512,3,128]{2,0,1:T(8,128)}) fusion(bf16[12,512,128]{2,1,0:T(8,128)(2,1)} %restore_step.1), kind=kLoop, calls=%fused_computation.10 | loop fusion | flops 3342336 | bytes 3932160 | tf_op jit(solution)/shard_map/transpose | solution.py:551

commit v5 on v4

--- a/solution.py
+++ b/solution.py
@@ -26,11 +26,11 @@
 
 
 def kernel(
-    blocks, owners, old_w, old_f, old_s, tok_in, cot_in,
+    blocks_in, owners_in, old_w, old_f, old_s, tok_in, cot_in,
     out,
     stage, xs, xr, mom, yx, swp, fin, wall, tok, cot, part, part_in, sgr, grd, r1, r2, ysum, r4, zed,
-    sel_a, sel_b, perm, perm64, perm128,
-    ssem, rsem, lsem,
+    sel_a, sel_b, perm, perm64, perm128, blocks, owners, moved,
+    ssem, rsem, lsem, osem,
 ):
     z, y, c, x = (lax.axis_index(a) for a in ("z", "y", "c", "x"))
     step4 = lambda v, d: lax.rem(v + d + 4, 4)
@@ -76,6 +76,7 @@
         local.append(d)
         return d
 
+    few = [load(blocks_in, blocks), load(owners_in, owners)]
     loads = [load(olds[k // 3].at[k % 3], stage.at[k]) for k in range(9)]
     quarter = pl.ds(pl.multiple_of(x * 4096, 4096), 4096)
     tload = []
@@ -85,6 +86,9 @@
         tload.append(load(cot_in.at[rows, quarter], cot.at[2 * c + mb, pl.ds(0, 240)]))
     tok[:, 240:, :] = jnp.zeros((4, 16, 4096), BF)
     cot[:, 240:, :] = jnp.zeros((4, 16, 4096), BF)
+
+    for d in few:
+        d.wait()
 
     shape = (16, 64)
     row, col = iota(shape, 0), iota(shape, 1)
@@ -358,7 +362,8 @@
                 deliver(swp.at[k, u, h], u, h, k)
 
     def owned(k):
-        out[k] = dot(perm128[...], fin[k].reshape(128, 512)).T.astype(BF)
+        moved[k] = dot(perm128[...], fin[k].reshape(128, 512)).T.astype(BF)
+        pltpu.make_async_copy(moved.at[k], out.at[k], osem).start()
 
     def mland(k):
         landed(k)
@@ -370,112 +375,113 @@
 
     part_in[:, :, 240:, :] = jnp.zeros((3, 3, 16, 256), BF)
     pack_w(1)
+    ag1(0)
+    pack_w(2)
+    mpack(6)
+    ag1(1)
+    ag2(0, 0, 3)
+    mpack(3)
+    ag2(0, 1, 3)
+    ag2(1, 0, 3)
+    ag2(1, 1, 1)
+    ag2(1, 1, 2)
+    ag2(1, 0, 2)
+    ag2(1, 1, 3)
+    ag2(1, 0, 1)
     mpack(4)
-    mpack(6)
+    fw(1, 0, 0)
+    ag2(0, 0, 1)
     mpack(5)
-    ag1(0)
-    ag1(1)
-    ag2(1, 0, 2)
-    ag2(1, 1, 1)
-    ag2(1, 0, 3)
     ag2(0, 1, 1)
-    ag2(1, 1, 3)
-    mpack(3)
-    ag2(1, 0, 1)
-    ag2(1, 1, 2)
-    ag2(0, 1, 2)
-    ag2(0, 1, 3)
-    pack_w(2)
-    ag2(0, 0, 2)
-    ag2(0, 0, 3)
-    ag2(0, 0, 1)
-    fw(1, 0, 3)
     fw(1, 1, 0)
     fw(1, 1, 1)
+    ag2(0, 1, 2)
+    ag2(0, 0, 2)
+    fw(1, 0, 1)
+    fw(1, 1, 3)
+    fw(1, 1, 2)
+    fw(1, 0, 3)
+    mpack(7)
     fw(1, 0, 2)
-    mpack(7)
-    fw(1, 1, 3)
-    fw(1, 0, 1)
-    fw(1, 1, 2)
-    fw(1, 0, 0)
+    mpack(8)
+    fw(0, 0, 0)
+    fw(0, 1, 3)
     fw(0, 1, 0)
-    fw(0, 1, 3)
+    fw(0, 1, 1)
     fw(0, 0, 3)
-    fw(0, 1, 1)
-    fw(0, 0, 0)
+    fw(0, 0, 2)
     fw(0, 1, 2)
-    fw(0, 0, 2)
     fw(0, 0, 1)
     ag1(2)
-    mpack(8)
+    mpick(5)
     fwd(1)
-    mpick(5)
-    ag2(2, 0, 1)
-    mpick(8)
     fwd(0)
-    ag2(2, 1, 2)
+    ag2(2, 0, 2)
     ag2(2, 1, 1)
     ag2(2, 1, 3)
-    ag2(2, 0, 2)
+    ag2(2, 1, 2)
+    mpick(6)
     ag2(2, 0, 3)
+    ag2(2, 0, 1)
+    mpick(4)
+    fw(2, 0, 0)
+    fw(2, 1, 1)
+    mswap(1)
+    mpick(3)
+    fw(2, 1, 3)
+    fw(2, 1, 0)
+    fw(2, 0, 2)
+    fw(2, 0, 1)
+    mswap(5)
+    fw(2, 1, 2)
+    hid()
+    fw(2, 0, 3)
+    fwd(2)
+    mpick(8)
     mswap(0)
-    mpick(6)
-    fw(2, 0, 2)
-    fw(2, 1, 1)
-    fw(2, 0, 1)
-    fw(2, 0, 0)
-    fw(2, 1, 2)
-    fw(2, 1, 0)
-    mswap(5)
-    fw(2, 0, 3)
-    fw(2, 1, 3)
-    hid()
-    fwd(2)
-    mswap(1)
+    mswap(6)
+    bwd(2)
     mswap(8)
-    mland(5)
-    bwd(2)
+    dg(1)
+    mpick(7)
+    dg(0)
+    mswap(4)
     mswap(2)
-    dg(1)
-    dg(0)
-    mpick(7)
-    mswap(6)
     rs2(2, 0)
-    mpick(4)
-    mpick(3)
-    mland(1)
     rs2(2, 1)
-    mswap(4)
     mswap(7)
     bwd(1)
+    rs3(2, 1)
+    mland(1)
     rs3(2, 0)
-    rs3(2, 1)
     bwd(0)
+    rs2(1, 0)
     rs2(1, 1)
-    rs2(1, 0)
+    mland(0)
+    rs2(0, 0)
+    mland(4)
     rs2(0, 1)
-    rs2(0, 0)
+    mland(7)
+    rs5(2, 1)
     rs3(1, 0)
-    rs5(2, 0)
-    mland(2)
     rs3(1, 1)
     rs3(0, 1)
     rs3(0, 0)
-    mland(4)
-    rs5(2, 1)
+    mland(6)
+    mland(2)
+    rs5(2, 0)
     mswap(3)
+    rs5(1, 0)
+    mland(5)
+    mland(8)
     rs5(1, 1)
-    rs5(1, 0)
-    mland(0)
-    mland(8)
-    mland(6)
-    mland(7)
     rs5(0, 1)
     rs5(0, 0)
     upd(2)
     mland(3)
     upd(1)
     upd(0)
+    pltpu.make_async_copy(moved, out, osem).wait()
     left(tok.at[pl.ds(0, 3), pl.ds(0, 240)], "gather")
     left(xs.at[:, pl.ds(0, 3)], "x")
     left(part_in.at[:, :, pl.ds(0, 240)], "part")
@@ -499,14 +505,12 @@
 
 def on_device(old_weights, old_first, old_second, old_blocks, owner_map, inputs, cotangent):
     any_ = pl.BlockSpec(memory_space=pl.ANY)
-    smem = pl.BlockSpec(memory_space=pltpu.SMEM)
-    vmem = pl.BlockSpec(memory_space=pltpu.VMEM)
     V = pltpu.VMEM
     states = pl.pallas_call(
         kernel,
         out_shape=jax.ShapeDtypeStruct((12, 512, 128), BF),
-        in_specs=[smem, smem, any_, any_, any_, any_, any_],
-        out_specs=vmem,
+        in_specs=[any_, any_, any_, any_, any_, any_, any_],
+        out_specs=any_,
         scratch_shapes=[
             V((9, 8, 16384), F32),
             V((9, 4, 16, 2048), BF),
@@ -532,9 +536,13 @@
             V((256, 256), BF),
             V((64, 64), BF),
             V((128, 128), BF),
+            pltpu.SMEM((128,), jnp.int32),
+            pltpu.SMEM((4, 128), jnp.int32),
+            V((12, 512, 128), BF),
             pltpu.SemaphoreType.DMA((10,)),
             pltpu.SemaphoreType.DMA((NS,)),
-            pltpu.SemaphoreType.DMA((13,)),
+            pltpu.SemaphoreType.DMA((15,)),
+            pltpu.SemaphoreType.DMA,
         ],
         compiler_params=pltpu.CompilerParams(
             collective_id=0, has_side_effects=True, vmem_limit_bytes=64 * 1024 * 1024

time: 122 us -> 121 us (level)
    pallas_call x1, Pallas kernels: 118 us -> 117 us  [on_device(): pl.pallas_call(kernel, out_shape=jax.ShapeDtypeStruct((12, 512, 128), BF)...]
where the time goes in v5:
time: 121 us; the launch traced here: 120 us
  Pallas kernels  117 us (97%)
  other arithmetic  3.15 us (3%)
    pallas_call x1, Pallas kernels, on_device(): pl.pallas_call(kernel, out_shape=jax.ShapeDtypeStruct((12, 512, 128), BF)...  117 us
    transpose x1, other arithmetic, on_device(): return tuple((jnp.transpose(o, (1, 0, 2)) for o in (w, first, second)))  3.15 us

profile of v5, /device:TPU:0, one launch (start us, length us, event | category | flops | bytes accessed | tf_op | source)
XLA Modules:
  0.0 120.4 jit_solution(8117202563333763490)
XLA Ops:
  0.6 116.6 %restore_step.1 = bf16[12,512,128]{2,1,0:T(8,128)(2,1)} custom-call(s32[128]{0:T(128)} %blocks_in.1, s32[4,128]{1,0:T(4,128)} %bitcast.11, f32[3,8,16384]{2,1,0:T(8,128)} %old_w.1, f32[3,8,16384]{2,1,0:T(8,128)} %old_f.1, f32[3,8,16384]{2,1,0:T(8,128)} %old_s.1, bf16[480,4096]{1,0:T(8,128)(2,1)} %bitcast.10, bf16[480,16384]{1,0:T(8,128)(2,1)} %bitcast.9), custom_call_target="tpu_custom_call" | custom-call | tf_op jit(solution)/shard_map/restore_step/pallas_call | solution.py:509
  117.3 3.1 %fusion.6 = (f32[512,3,128]{2,0,1:T(8,128)}, f32[512,3,128]{2,0,1:T(8,128)}, f32[512,3,128]{2,0,1:T(8,128)}) fusion(bf16[12,512,128]{2,1,0:T(8,128)(2,1)} %restore_step.1), kind=kLoop, calls=%fused_computation.10 | loop fusion | flops 3342336 | bytes 3932160 | tf_op jit(solution)/shard_map/transpose | solution.py:559

commit v6 on v5

--- a/solution.py
+++ b/solution.py
@@ -267,23 +267,32 @@
         acts = acts_of(m)
         arrived(sgr.at[m, pl.ds(0, 3)], "share", m)
 
-        def body(n, carry):
-            cols = pl.ds(pl.multiple_of(n * 512, 512), 512)
+        def block(yy, h):
+            cols = pl.ds(pl.multiple_of(yy * 1024 + h * 512, 512), 512)
             left = jnp.concatenate([sgr[m, b] for b in range(4)], axis=1)
             right = acts[:, :, cols].reshape(1024, 512)
-            res = dot(left, right).astype(BF).reshape(4, 64, 512)
-            grd[m, lax.rem(n, 2), n // 2] = res
-            return carry
-
-        lax.fori_loop(0, 8, body, 0)
-        for h in range(2):
+            grd[m, h, yy] = dot(left, right).astype(BF).reshape(4, 64, 512)
+
+        def blocks(first, n, h):
+            def body(i, carry):
+                block(step4(first, i), h)
+                return carry
+
+            lax.fori_loop(0, n, body, 0)
+
+        def send(h, half):
             far = at2(h, 2)
-            for half in range(2):
-                if h == 0:
-                    src = grd.at[m, h, pl.ds(2 * half, 2), far]
-                else:
-                    src = grd.at[m, h, far, pl.ds(2 * half, 2)]
-                copy(src, r1.at[m, h, half], ring2(h, 1 if half == 0 else -1), "r1", m, h)
+            pair = pl.ds(2 * half, 2)
+            src = grd.at[m, h, pair, far] if h == 0 else grd.at[m, h, far, pair]
+            copy(src, r1.at[m, h, half], ring2(h, 1 if half == 0 else -1), "r1", m, h)
+
+        block(step4(y, 2), 1)
+        send(1, 0)
+        send(1, 1)
+        blocks(0, 4, 0)
+        send(0, 0)
+        send(0, 1)
+        blocks(y + 3, 3, 1)
 
     def gref(m, h, p, q):
         return (m, h, q, p) if h == 0 else (m, h, p, q)

time: 121 us -> 119 us (0.983)
  Pallas kernels: 117 us -> 115 us
    pallas_call x1, Pallas kernels: 117 us -> 115 us  [on_device(): pl.pallas_call(kernel, out_shape=jax.ShapeDtypeStruct((12, 512, 128), BF)...]
where the time goes in v6:
time: 119 us
  Pallas kernels  115 us (97%)
  other arithmetic  3.15 us (3%)
    pallas_call x1, Pallas kernels, on_device(): pl.pallas_call(kernel, out_shape=jax.ShapeDtypeStruct((12, 512, 128), BF)...  115 us
    transpose x1, other arithmetic, on_device(): return tuple((jnp.transpose(o, (1, 0, 2)) for o in (w, first, second)))  3.15 us

profile of v6, /device:TPU:0, one launch (start us, length us, event | category | flops | bytes accessed | tf_op | source)
XLA Modules:
  0.0 118.9 jit_solution(15661380960127508100)
XLA Ops:
  0.6 115.2 %restore_step.1 = bf16[12,512,128]{2,1,0:T(8,128)(2,1)} custom-call(s32[128]{0:T(128)} %blocks_in.1, s32[4,128]{1,0:T(4,128)} %bitcast.11, f32[3,8,16384]{2,1,0:T(8,128)} %old_w.1, f32[3,8,16384]{2,1,0:T(8,128)} %old_f.1, f32[3,8,16384]{2,1,0:T(8,128)} %old_s.1, bf16[480,4096]{1,0:T(8,128)(2,1)} %bitcast.10, bf16[480,16384]{1,0:T(8,128)(2,1)} %bitcast.9), custom_call_target="tpu_custom_call" | custom-call | tf_op jit(solution)/shard_map/restore_step/pallas_call | solution.py:518
  115.8 3.1 %fusion.6 = (f32[512,3,128]{2,0,1:T(8,128)}, f32[512,3,128]{2,0,1:T(8,128)}, f32[512,3,128]{2,0,1:T(8,128)}) fusion(bf16[12,512,128]{2,1,0:T(8,128)(2,1)} %restore_step.1), kind=kLoop, calls=%fused_computation.10 | loop fusion | flops 3342336 | bytes 3932160 | tf_op jit(solution)/shard_map/transpose | solution.py:568
